TPU v7x, 32 devices: a whole 2x2x4 slice. The times are simulated.
32 devices in a mesh: dp: 16 (over z, x, core), tensor: 2 (over y).
Axes of the slice: x: 2, y: 2, z: 4, core: 2. Of those that a mesh axis runs over, the one named last changes fastest.
Arguments:
- tokens: bfloat16 [6144, 1024], P('dp', 'tensor'), may hold values from -6 to 6
- cotangent: bfloat16 [6144, 1024], P('dp', 'tensor'), may hold values from -6 to 6
- attn_gain: float32 [1024], replicated, may hold values from 0.5 to 1.5
- query_weight: bfloat16 [1024, 2048], P(None, 'tensor'), may hold values from -0.1875 to 0.1875
- key_matrix: bfloat16 [1024, 1024], P(None, 'tensor'), may hold values from -0.1875 to 0.1875
- value_matrix: bfloat16 [1024, 1024], P(None, 'tensor'), may hold values from -0.1875 to 0.1875
- query_gain: float32 [128], replicated, may hold values from 1 to 2
- key_norm_gain: float32 [128], replicated, may hold values from 1 to 2
- out_weight: bfloat16 [2048, 1024], P('tensor'), may hold values from -0.75 to 0.75
- mlp_gain: float32 [1024], replicated, may hold values from 0.5 to 1.5
- gate_weight: bfloat16 [1024, 3072], P(None, 'tensor'), may hold values from -0.1875 to 0.1875
- up_weight: bfloat16 [1024, 3072], P(None, 'tensor'), may hold values from -0.1875 to 0.1875
- down_weight: bfloat16 [3072, 1024], P('tensor'), may hold values from -0.21875 to 0.21875
Outputs:
- layer_out: bfloat16 [6144, 1024], P('dp', 'tensor')
- input_grad: bfloat16 [6144, 1024], P('dp', 'tensor')
- attn_gain_grad: float32 [1024], replicated
- query_weight_grad: float32 [1024, 2048], P(None, 'tensor')
- key_weight_grad: float32 [1024, 1024], P(None, 'tensor')
- value_weight_grad: float32 [1024, 1024], P(None, 'tensor')
- query_gain_grad: float32 [128], replicated
- key_gain_grad: float32 [128], replicated
- out_weight_grad: float32 [2048, 1024], P('tensor')
- mlp_gain_grad: float32 [1024], replicated
- gate_weight_grad: float32 [1024, 3072], P(None, 'tensor')
- up_weight_grad: float32 [1024, 3072], P(None, 'tensor')
- down_weight_grad: float32 [3072, 1024], P('tensor')
All inputs are finite; a program needn't handle non-finite values.
Results may differ from a plain program's by a relative error of at most 0.025.
Values may be sent and summed in bfloat16 or wider, within the bound.
No kernel may reach another device: no remote copies, remote signals or barrier semaphores. Data moves between devices by JAX's collectives and lax.ppermute only.
A program may use at most 192 MiB of HBM per device.

v0:
```python
import jax
import jax.numpy as jnp
from jax import lax
from jax.sharding import PartitionSpec as P

HEAD_SIZE = 128
SEQUENCE_LENGTH = 384
BLOCK = 384


epsilon = 1e-06
rope_base = 1000000.0


def norm_rows(values, gain_vec):
    return values * lax.rsqrt(jnp.mean(values * values, -1, keepdims=True) + epsilon) * gain_vec


def rotary_embed(values, token_positions):
    half_width = values.shape[-1] // 2
    steps_up = jnp.arange(half_width, dtype=jnp.float32) * (2.0 / values.shape[-1])
    frequency = rope_base ** (-steps_up)
    angle_grid = token_positions.astype(jnp.float32)[:, None] * frequency[None, :]
    cosine = jnp.cos(angle_grid)[:, None, :]
    sine_part = jnp.sin(angle_grid)[:, None, :]
    front_half = values[..., :half_width]
    back_half = values[..., half_width:]
    return jnp.concatenate(
        [front_half * cosine - back_half * sine_part, back_half * cosine + front_half * sine_part],
        -1,
    )


def dot_plain(left, right):
    return jnp.dot(left, right, preferred_element_type=jnp.float32)


def dot_rows(left, right):
    return lax.dot_general(
        left, right, (((0,), (0,)), ((), ())), preferred_element_type=jnp.float32
    )


def dot_cols(left, right):
    return lax.dot_general(
        left, right, (((1,), (1,)), ((), ())), preferred_element_type=jnp.float32
    )


def per_device(
    tokens,
    cotangent,
    attn_gain,
    query_weight,
    key_matrix,
    value_matrix,
    query_gain,
    key_norm_gain,
    out_weight,
    mlp_gain,
    gate_weight,
    up_weight,
    down_weight,
):
    token_full, cotan_full = (
        lax.all_gather(tokens, "tensor", axis=1, tiled=True),
        lax.all_gather(cotangent, "tensor", axis=1, tiled=True),
    )
    total_rows, model_width = token_full.shape
    shard_width = tokens.shape[1]
    offset = lax.axis_index("tensor") * shard_width
    sequence_count = total_rows // SEQUENCE_LENGTH
    local_query = query_weight.shape[1] // HEAD_SIZE
    local_kv = key_matrix.shape[1] // HEAD_SIZE
    heads_per_group = local_query // local_kv
    score_scale = HEAD_SIZE ** (-0.5)
    token_wide = token_full.astype(jnp.float32)
    inv_one = lax.rsqrt(jnp.mean(token_wide * token_wide, -1, keepdims=True) + epsilon)
    normed_one = (token_wide * inv_one * attn_gain).astype(jnp.bfloat16)
    query_raw = dot_plain(normed_one, query_weight)
    key_projected = dot_plain(normed_one, key_matrix)
    value_lowered = dot_plain(normed_one, value_matrix).astype(jnp.bfloat16)
    token_positions = jnp.arange(total_rows, dtype=jnp.int32) % SEQUENCE_LENGTH

    def query_path(raw_vals, gain_vec):
        return (
            rotary_embed(
                norm_rows(raw_vals.reshape(total_rows, local_query, HEAD_SIZE), gain_vec),
                token_positions,
            )
            * score_scale
        )

    def key_path(raw_vals, gain_vec):
        return rotary_embed(
            norm_rows(raw_vals.reshape(total_rows, local_kv, HEAD_SIZE), gain_vec), token_positions
        )

    query_rotated, query_back = jax.vjp(query_path, query_raw, query_gain)
    key_rotated, key_back = jax.vjp(key_path, key_projected, key_norm_gain)
    query_low = query_rotated.astype(jnp.bfloat16).reshape(
        sequence_count, SEQUENCE_LENGTH, local_kv, heads_per_group, HEAD_SIZE
    )
    key_low = key_rotated.astype(jnp.bfloat16).reshape(
        sequence_count, SEQUENCE_LENGTH, local_kv, HEAD_SIZE
    )
    value_seq = value_lowered.reshape(sequence_count, SEQUENCE_LENGTH, local_kv, HEAD_SIZE)

    def block_scores(block_index):
        row_start = block_index * BLOCK
        row_stop = row_start + BLOCK
        scores = jnp.einsum(
            "sqhgd,skhd->shgqk", query_low, key_low, preferred_element_type=jnp.float32
        )
        allowed = jnp.arange(row_stop)[None, :] <= (row_start + jnp.arange(BLOCK))[:, None]
        return jnp.where(allowed, scores, -1e30)

    block_index = 0
    row_stop = (block_index + 1) * BLOCK
    scores = block_scores(block_index)
    top_score = jnp.max(scores, -1, keepdims=True)
    raised = jnp.exp(scores - top_score)
    prob_total = jnp.sum(raised, -1, keepdims=True)
    attn_prob = raised / prob_total
    log_totals = [top_score + jnp.log(prob_total)]
    outputs = jnp.einsum(
        "shgqk,skhd->sqhgd",
        attn_prob.astype(jnp.bfloat16),
        value_seq,
        preferred_element_type=jnp.float32,
    )
    attn_low = outputs.reshape(total_rows, local_query * HEAD_SIZE).astype(jnp.bfloat16)
    branch_part = dot_plain(attn_low, out_weight)
    branch_share = lax.psum_scatter(branch_part, "tensor", scatter_dimension=1, tiled=True)
    middle_share = tokens.astype(jnp.float32) + branch_share
    mlp_gain_share = lax.dynamic_slice_in_dim(mlp_gain, offset, shard_width, 0)
    middle_full = lax.all_gather(middle_share, "tensor", axis=1, tiled=True)
    inv_two = lax.rsqrt(jnp.mean(middle_full * middle_full, -1, keepdims=True) + epsilon)
    normed_two = (middle_full * inv_two * mlp_gain).astype(jnp.bfloat16)
    gate_val = dot_plain(normed_two, gate_weight)
    up_val = dot_plain(normed_two, up_weight)
    sigmoid_gate = jax.nn.sigmoid(gate_val)
    silu_gate = gate_val * sigmoid_gate
    hidden = (silu_gate * up_val).astype(jnp.bfloat16)
    mlp_part = dot_plain(hidden, down_weight)
    mlp_share = lax.psum_scatter(
        mlp_part.astype(jnp.bfloat16), "tensor", scatter_dimension=1, tiled=True
    ).astype(jnp.float32)
    layer_out = (middle_share + mlp_share).astype(jnp.bfloat16)
    down_wgrad = dot_rows(hidden, cotan_full)
    hidden_grad = dot_cols(cotan_full, down_weight)
    gate_grad = (
        hidden_grad * up_val * sigmoid_gate * (1.0 + gate_val * (1.0 - sigmoid_gate))
    ).astype(jnp.bfloat16)
    up_grad = (hidden_grad * silu_gate).astype(jnp.bfloat16)
    gate_wgrad = dot_rows(normed_two, gate_grad)
    up_wgrad = dot_rows(normed_two, up_grad)
    normed_grad_part = dot_cols(gate_grad, gate_weight) + dot_cols(up_grad, up_weight)
    normed_grad = lax.psum_scatter(
        normed_grad_part.astype(jnp.bfloat16), "tensor", scatter_dimension=1, tiled=True
    ).astype(jnp.float32)
    unit_two = middle_share * inv_two
    scaled_two = normed_grad * mlp_gain_share
    row_part_two = jnp.sum(scaled_two * unit_two, -1)
    gain_part_two = lax.dynamic_update_slice_in_dim(
        jnp.zeros((model_width,), jnp.float32), jnp.sum(normed_grad * unit_two, 0), offset, 0
    )
    row_total_two, mlp_gain_grad = lax.psum((row_part_two, gain_part_two), "tensor")
    middle_grad = cotangent.astype(jnp.float32) + inv_two * (
        scaled_two - unit_two * row_total_two[:, None] / model_width
    )
    branch_low = lax.all_gather(middle_grad.astype(jnp.bfloat16), "tensor", axis=1, tiled=True)
    out_wgrad = dot_rows(attn_low, branch_low)
    attn_grad = (
        dot_cols(branch_low, out_weight)
        .astype(jnp.bfloat16)
        .reshape(sequence_count, SEQUENCE_LENGTH, local_kv, heads_per_group, HEAD_SIZE)
    )
    key_grad = jnp.zeros((sequence_count, SEQUENCE_LENGTH, local_kv, HEAD_SIZE), jnp.float32)
    value_grad = jnp.zeros((sequence_count, SEQUENCE_LENGTH, local_kv, HEAD_SIZE), jnp.float32)
    block_index = 0
    row_start = block_index * BLOCK
    row_stop = row_start + BLOCK
    scores = block_scores(block_index)
    attn_prob = jnp.exp(scores - log_totals[block_index])
    value_grad = value_grad.at[:, :row_stop].add(
        jnp.einsum(
            "shgqk,sqhgd->skhd",
            attn_prob.astype(jnp.bfloat16),
            attn_grad,
            preferred_element_type=jnp.float32,
        )
    )
    prob_grad = jnp.einsum(
        "sqhgd,skhd->shgqk", attn_grad, value_seq, preferred_element_type=jnp.float32
    )
    row_dot = jnp.sum(prob_grad * attn_prob, -1, keepdims=True)
    score_grad = (attn_prob * (prob_grad - row_dot)).astype(jnp.bfloat16)
    query_grads = jnp.einsum(
        "shgqk,skhd->sqhgd", score_grad, key_low, preferred_element_type=jnp.float32
    )
    key_grad = key_grad.at[:, :row_stop].add(
        jnp.einsum("shgqk,sqhgd->skhd", score_grad, query_low, preferred_element_type=jnp.float32)
    )
    query_rot_grad = query_grads.reshape(total_rows, local_query, HEAD_SIZE)
    query_raw_grad, query_gain_grad = query_back(query_rot_grad)
    key_raw_grad, key_gain_grad = key_back(key_grad.reshape(total_rows, local_kv, HEAD_SIZE))
    query_low_grad = query_raw_grad.astype(jnp.bfloat16)
    key_low_grad = key_raw_grad.astype(jnp.bfloat16)
    value_low_grad = value_grad.reshape(total_rows, local_kv * HEAD_SIZE).astype(jnp.bfloat16)
    query_wgrad = dot_rows(normed_one, query_low_grad)
    key_wgrad = dot_rows(normed_one, key_low_grad)
    value_wgrad = dot_rows(normed_one, value_low_grad)
    normed_one_grad = (
        dot_cols(query_low_grad, query_weight)
        + dot_cols(key_low_grad, key_matrix)
        + dot_cols(value_low_grad, value_matrix)
    )
    input_share_grad = lax.psum_scatter(
        normed_one_grad.astype(jnp.bfloat16), "tensor", scatter_dimension=1, tiled=True
    ).astype(jnp.float32)
    unit_one = lax.dynamic_slice_in_dim(token_wide, offset, shard_width, 1) * inv_one
    scaled_one = input_share_grad * lax.dynamic_slice_in_dim(attn_gain, offset, shard_width, 0)
    row_part_one = jnp.sum(scaled_one * unit_one, -1)
    gain_part_one = lax.dynamic_update_slice_in_dim(
        jnp.zeros((model_width,), jnp.float32), jnp.sum(input_share_grad * unit_one, 0), offset, 0
    )
    row_total_one, attn_gain_grad, query_gain_grad, key_gain_grad = lax.psum(
        (row_part_one, gain_part_one, query_gain_grad, key_gain_grad), "tensor"
    )
    input_grad = (
        middle_grad + inv_one * (scaled_one - unit_one * row_total_one[:, None] / model_width)
    ).astype(jnp.bfloat16)
    (
        attn_gain_grad,
        query_wgrad,
        key_wgrad,
        value_wgrad,
        query_gain_grad,
        key_gain_grad,
        out_wgrad,
        mlp_gain_grad,
        gate_wgrad,
        up_wgrad,
        down_wgrad,
    ) = (
        lax.psum(attn_gain_grad.astype(jnp.bfloat16), "dp").astype(jnp.float32),
        lax.psum(query_wgrad.astype(jnp.bfloat16), "dp").astype(jnp.float32),
        lax.psum(key_wgrad.astype(jnp.bfloat16), "dp").astype(jnp.float32),
        lax.psum(value_wgrad.astype(jnp.bfloat16), "dp").astype(jnp.float32),
        lax.psum(query_gain_grad.astype(jnp.bfloat16), "dp").astype(jnp.float32),
        lax.psum(key_gain_grad.astype(jnp.bfloat16), "dp").astype(jnp.float32),
        lax.psum(out_wgrad.astype(jnp.bfloat16), "dp").astype(jnp.float32),
        lax.psum(mlp_gain_grad.astype(jnp.bfloat16), "dp").astype(jnp.float32),
        lax.psum(gate_wgrad.astype(jnp.bfloat16), "dp").astype(jnp.float32),
        lax.psum(up_wgrad.astype(jnp.bfloat16), "dp").astype(jnp.float32),
        lax.psum(down_wgrad.astype(jnp.bfloat16), "dp").astype(jnp.float32),
    )
    return (
        layer_out,
        input_grad,
        attn_gain_grad,
        query_wgrad,
        key_wgrad,
        value_wgrad,
        query_gain_grad,
        key_gain_grad,
        out_wgrad,
        mlp_gain_grad,
        gate_wgrad,
        up_wgrad,
        down_wgrad,
    )


def solution(mesh):
    return jax.shard_map(
        per_device,
        mesh=mesh,
        in_specs=(
            P("dp", "tensor"),
            P("dp", "tensor"),
            P(),
            P(None, "tensor"),
            P(None, "tensor"),
            P(None, "tensor"),
            P(),
            P(),
            P("tensor", None),
            P(),
            P(None, "tensor"),
            P(None, "tensor"),
            P("tensor", None),
        ),
        out_specs=(
            P("dp", "tensor"),
            P("dp", "tensor"),
            P(),
            P(None, "tensor"),
            P(None, "tensor"),
            P(None, "tensor"),
            P(),
            P(),
            P("tensor", None),
            P(),
            P(None, "tensor"),
            P(None, "tensor"),
            P("tensor", None),
        ),
        check_vma=False,
    )
```

profile of v0, /device:TPU:0, one launch (start us, length us, event | category | flops | bytes accessed | tf_op | source)
XLA Modules:
  0.0 568.5 jit_solution(11189757606620563507)
XLA Ops:
  7.3 13.1 %all_gather.12 = bf16[384,1024]{1,0:T(8,128)(2,1)S(1)} all-gather(bf16[384,512]{1,0:T(8,128)(2,1)} %param.21), channel_id=1, replica_groups=mesh['dp'=16,'tensor'=2] {'tensor'}, dimensions={1}, use_global_device_ids=true | all-gather | bytes 1179648 | tf_op jit(solution)/shard_map/all_gather | solution.py:66
  24.7 1.9 multiply_multiply_fusion
  28.1 1.4 copy.134
  29.5 1.4 copy.133
  31.5 1.5 fusion.60
  33.0 2.3 reshape.331
  35.3 2.3 multiply_reduce_fusion.6
  38.7 1.4 fusion.46
  41.9 1.4 convolution_convert_fusion.9
  43.3 1.8 reshape.330
  45.1 2.4 fusion.18
  50.7 1.5 fusion.19
  53.1 2.1 fusion.62
  55.3 27.6 %reduce-scatter.5.cloned.1.call-done = f32[384,512]{1,0:T(8,128)} async-done(((f32[384,1024]{1,0:T(8,128)}), f32[384,512]{1,0:T(8,128)}) %reduce-scatter.5.cloned.1.call-update) | async-done | bytes 786448 | tf_op jit(solution)/shard_map/reduce_scatter | solution.py:134
  83.0 2.2 convert_add_fusion
  85.3 15.7 %all_gather.14 = bf16[384,1024]{1,0:T(8,128)(2,1)} all-gather(bf16[384,512]{1,0:T(8,128)(2,1)} %param.22), channel_id=1, replica_groups=mesh['dp'=16,'tensor'=2] {'tensor'}, dimensions={1}, use_global_device_ids=true | all-gather | bytes 1179648 | tf_op jit(solution)/shard_map/all_gather | solution.py:67
  101.0 13.8 %all-gather.2.cloned.1.call-done = f32[384,1024]{1,0:T(8,128)} async-done(((f32[384,512]{1,0:T(8,128)}), f32[384,1024]{1,0:T(8,128)}) %all-gather.2.cloned.1.call-update) | async-done | bytes 1572880 | tf_op jit(solution)/shard_map/all_gather | solution.py:137
  114.8 1.7 multiply_reduce_fusion.2
  116.9 3.6 fusion.63
  120.5 1.4 fusion.64
  122.0 3.3 multiply_convert_fusion
  125.3 1.4 fusion.65
  126.7 2.3 add_convert_fusion.1
  129.9 17.8 %reduce-scatter.9.cloned.1.call-done = bf16[384,512]{1,0:T(8,128)(2,1)} async-done(((bf16[384,1024]{1,0:T(8,128)(2,1)}), bf16[384,512]{1,0:T(8,128)(2,1)}) %reduce-scatter.9.cloned.1.call-update) | async-done | bytes 393232 | tf_op jit(solution)/shard_map/reduce_scatter | solution.py:159
  147.6 2.2 fusion.39
  149.8 4.9 psum.119
  154.8 1.8 fusion.59
  156.6 10.6 %all_gather.15 = bf16[384,1024]{1,0:T(8,128)(2,1)S(1)} all-gather(bf16[384,512]{1,0:T(8,128)(2,1)S(1)} %fusion.59), channel_id=1, replica_groups=mesh['dp'=16,'tensor'=2] {'tensor'}, dimensions={1}, use_global_device_ids=true | all-gather | bytes 1179648 | tf_op jit(solution)/shard_map/all_gather | solution.py:172
  168.1 1.9 convolution_convert_fusion.8
  170.0 2.3 copy.173
  172.3 4.1 fusion
  178.8 1.6 convolution_bitcast_fusion.1
  180.4 1.8 fusion.25
  183.5 2.8 copy.172
  186.3 2.8 copy.171
  189.0 2.4 multiply_add_fusion.1
  191.5 2.8 multiply_reduce_fusion
  196.1 3.3 fusion.17
  200.3 2.2 fusion.43
  206.3 2.1 fusion.66
  208.5 1.5 add_convert_fusion
  210.1 5.1 convolution_convert_fusion.2
  215.2 2.3 convolution_convert_fusion.7
  217.8 5.1 convolution_convert_fusion.1
  222.9 3.5 convolution_convert_fusion
  226.5 1.9 convolution_convert_fusion.6
  228.3 1.9 convolution_convert_fusion.5
  230.2 2.6 convolution_convert_fusion.3
  232.8 2.7 convolution_convert_fusion.4
  235.6 2.5 convert_element_type.217
  239.3 1.4 dynamic_update_slice.7
  240.7 2.2 fusion.40
  243.5 1.4 dynamic_update_slice.6
  244.9 8.5 %all-reduce.4 = (f32[384]{0:T(512)}, bf16[1024]{0:T(1024)(128)(2,1)}, bf16[128]{0:T(256)(128)(2,1)}, bf16[128]{0:T(256)(128)(2,1)}, bf16[1024]{0:T(1024)(128)(2,1)}) all-reduce(f32[384]{0:T(512)} %get-tuple-element.58, f32[1024]{0:T(1024)} %dynamic_update_slice.6, ...), channel_id=1, replica_groups=mesh['dp'=16,'tensor'=2] {'tensor'}, use_global_device_ids=true, to_apply=%region_16.17 | all-reduce | flops 2688 | bytes 16896 | tf_op jit(solution)/shard_map/psum | solution.py:228
  253.4 32.5 %all-reduce.5 = (bf16[1024]{0:T(1024)(128)(2,1)}, bf16[128]{0:T(256)(128)(2,1)}, bf16[128]{0:T(256)(128)(2,1)}, bf16[1024]{0:T(1024)(128)(2,1)}) all-reduce(bf16[1024]{0:T(1024)(128)(2,1)} %get-tuple-element.62, bf16[128]{0:T(256)(128)(2,1)} %get-tuple-element.63, ...), channel_id=1, replica_groups=mesh['dp'=16,'tensor'=2] {'dp'}, use_global_device_ids=true, to_apply=%region_19.20 | all-reduce | flops 2304 | bytes 9216 | tf_op jit(solution)/shard_map/psum | solution.py:247
  290.8 3.1 fusion.35
  293.9 245.7 %all-reduce.9.cloned.1.call-done = (bf16[1024,1024]{1,0:T(8,128)(2,1)}, bf16[1024,512]{1,0:T(8,128)(2,1)}, bf16[1024,512]{1,0:T(8,128)(2,1)}, bf16[1024,1024]{1,...) async-done(((bf16[1024,1024]{1,0:T(8,128)(2,1)}, bf16[1024,512]{1,0:T(8,128)(2,1)}, ...) | async-done | bytes 15728656 | tf_op jit(solution)/shard_map/psum | solution.py:248
  539.6 4.2 convert_element_type.255
  543.8 1.6 convert_element_type.257
  545.4 1.6 convert_element_type.259
  547.8 2.5 convert_element_type.265
  550.8 3.6 convert_element_type.269
  554.4 3.6 convert_element_type.271
  558.0 3.5 convert_element_type.273
  (201 shorter events, 34.0 us)
Async XLA Ops:
  7.2 114.8 %copy-start = (bf16[1536,1024]{1,0:T(8,128)(2,1)S(1)}, bf16[1536,1024]{1,0:T(8,128)(2,1)}, u32[]{:S(2)}) copy-start(bf16[1536,1024]{1,0:T(8,128)(2,1)} %param.33) | copy-start | bytes 9437188
  7.2 13.5 %copy-start.60 = (f32[1024]{0:T(1024)S(1)}, f32[1024]{0:T(1024)}, u32[]{:S(2)}) copy-start(f32[1024]{0:T(1024)} %param.23) | copy-start | bytes 12292
  7.2 75.8 %reduce-scatter.5.cloned.1.call-start = ((), (), s32[]{:S(2)}) async-start(), calls=%async_computation.4 | async-start | bytes 2359296 | tf_op jit(solution)/shard_map/reduce_scatter | solution.py:134
  7.3 13.4 %copy-start.65 = (bf16[1024,1024]{1,0:T(8,128)(2,1)S(1)}, bf16[1024,1024]{1,0:T(8,128)(2,1)}, u32[]{:S(2)}) copy-start(bf16[1024,1024]{1,0:T(8,128)(2,1)} %param.24) | copy-start | bytes 6291460
  20.7 20.7 %copy-start.51 = (f32[384]{0:T(512)}, f32[384]{0:T(512)S(1)}, u32[]{:S(2)}) copy-start(f32[384]{0:T(512)S(1)} %add_rsqrt_fusion.1) | copy-start | bytes 4612
  22.1 2.5 copy-start.58
  29.5 1.4 copy-start.8
  29.5 2.0 copy-start.35
  33.0 5.6 copy-start.56
  38.6 1.5 copy-start.16
  40.1 1.7 copy-start.38
  45.1 2.5 copy-start.20
  45.1 2.5 copy-start.22
  48.5 2.2 copy-start.1
  48.5 2.2 copy-start.29
  49.4 2.8 copy-start.50
  50.7 2.4 copy-start.31
  55.3 59.5 %all-gather.2.cloned.1.call-start = ((), (), s32[]{:S(2)}) async-start(), calls=%async_computation.5 | async-start | bytes 2359296 | tf_op jit(solution)/shard_map/all_gather | solution.py:137
  85.2 31.3 %copy-start.55 = (f32[1024]{0:T(1024)S(1)}, f32[1024]{0:T(1024)}, u32[]{:S(2)}) copy-start(f32[1024]{0:T(1024)} %param.30) | copy-start | bytes 12292
  85.2 62.4 %reduce-scatter.9.cloned.1.call-start = ((), (), s32[]{:S(2)}) async-start(), calls=%async_computation.7 | async-start | bytes 1179648 | tf_op jit(solution)/shard_map/reduce_scatter | solution.py:159
  114.8 1.9 copy-start.14
  116.9 3.6 copy-start.46
  116.9 3.6 copy-start.64
  120.5 1.4 copy-start.42
  122.0 3.3 copy-start.63
  125.3 1.4 copy-start.69
  129.0 111.7 %reduce-scatter.11.cloned.1.call-start = ((), (), s32[]{:S(2)}) async-start(), calls=%async_computation.8 | async-start | bytes 1179648 | tf_op jit(solution)/shard_map/reduce_scatter | solution.py:219
  154.8 12.4 %copy-start.53 = (f32[384]{0:T(512)}, f32[384]{0:T(512)S(1)}, u32[]{:S(2)}) copy-start(f32[384]{0:T(512)S(1)} %psum.119) | copy-start | bytes 4612
  154.8 13.4 %copy-start.32 = (bf16[1024,1024]{1,0:T(8,128)(2,1)S(1)}, bf16[1024,1024]{1,0:T(8,128)(2,1)}, u32[]{:S(2)}) copy-start(bf16[1024,1024]{1,0:T(8,128)(2,1)} %param.29) | copy-start | bytes 6291460
  172.3 4.1 slice-start
  172.3 4.1 slice-start.1
  178.8 1.6 copy-start.18
  189.0 2.4 copy-start.3
  189.0 2.4 copy-start.25
  189.0 2.4 copy-start.59
  191.4 2.8 copy-start.4
  191.4 2.8 copy-start.5
  196.1 4.2 copy-start.66
  200.3 2.2 copy-start.11
  200.3 2.2 copy-start.17
  206.3 2.1 copy-start.33
  206.3 2.1 copy-start.39
  206.3 2.2 copy-start.49
  210.1 80.7 %reduce-scatter.7.cloned.1.call-start = ((), (), s32[]{:S(2)}) async-start(), calls=%async_computation.6 | async-start | bytes 1179648 | tf_op jit(solution)/shard_map/reduce_scatter | solution.py:146
  210.1 5.1 copy-start.67
  217.5 322.1 %all-reduce.9.cloned.1.call-start = ((), (), s32[]{:S(2)}) async-start(), calls=%async_computation.9 | async-start | bytes 31457280 | tf_op jit(solution)/shard_map/psum | solution.py:248
  217.7 5.2 copy-start.43
  217.7 5.2 copy-start.68
  222.9 3.5 copy-start.10
  222.9 3.5 copy-start.34
  222.9 3.5 copy-start.52
  222.9 3.5 copy-start.61
  228.3 1.9 copy-start.45
  228.3 1.9 copy-start.48
  230.2 2.6 copy-start.41
  235.5 2.5 copy-start.62
  235.6 55.2 %copy-start.19 = (bf16[384,512]{1,0:T(8,128)(2,1)S(1)}, bf16[384,512]{1,0:T(8,128)(2,1)}, u32[]{:S(2)}) copy-start(bf16[384,512]{1,0:T(8,128)(2,1)} %param.22) | copy-start | bytes 1179652
  235.6 55.2 %copy-start.54 = (f32[384]{0:T(512)S(1)}, f32[384]{0:T(512)}, u32[]{:S(2)}) copy-start(f32[384]{0:T(512)} %copy-done.53) | copy-start | bytes 4612
  539.6 4.2 copy-start.37
  543.8 1.6 copy-start.36
  545.4 2.3 copy-start.30
  547.8 3.0 copy-start.28
  550.8 3.6 copy-start.27
  554.4 3.6 copy-start.26
  (15 other events, 15.9 us)
Sparse Core Ops, SparseCore 0:
  55.4 27.5 reduce-scatter.4
  85.4 29.3 all-gather.1
  129.1 18.4 reduce-scatter.8
  210.2 17.4 reduce-scatter.10
  229.8 17.4 reduce-scatter.6
  253.9 285.7 all-reduce.8
where the time goes:
time: 578 us; the launch traced here: 568 us
  waiting for transfers between devices  305 us (53%)
  blocking collectives  85.3 us (15%)
  other arithmetic  66.2 us (11%)
  matrix products  61.6 us (11%)
  local copies, waits for them, and re-layouts  34.8 us (6%)
  between operations  15.1 us (3%)
    psum x1, waiting for transfers between devices, per_device(): lax.psum(query_wgrad.astype(jnp.bfloat16), 'dp').astype(jnp.float32)  246 us
    psum x1, blocking collectives, per_device(): lax.psum(attn_gain_grad.astype(jnp.bfloat16), 'dp').astype(jnp.float32)  32.5 us
    reduce_scatter x1, waiting for transfers between devices, per_device(): lax.psum_scatter(branch_part, 'tensor', scatter_dimension=1, tiled=True)  27.6 us
    dot_general x7, matrix products, dot_rows(): lax.dot_general(left, right, (((0,), (0,)), ((), ())), preferred_element_...  22.8 us
    reduce_scatter x1, waiting for transfers between devices, per_device(): lax.psum_scatter(normed_grad_part.astype(jnp.bfloat16), 'tensor', scatter...  17.8 us
    all_gather x1, blocking collectives, per_device(): lax.all_gather(cotangent, 'tensor', axis=1, tiled=True)  15.7 us
    unnamed x149, local copies, waits for them, and re-layouts  15.6 us
    dot_general x7, matrix products, dot_cols(): lax.dot_general(left, right, (((1,), (1,)), ((), ())), preferred_element_...  14.7 us
  transfers between devices with their start and end apart: 6, of which 4 were waited for; matrix products, arithmetic and copies ran while one was open for 8% of the time, Pallas kernels for 0%

commit v1 on v0

v1 whole, which is shorter than its diff:
```python
import functools

import jax
import jax.numpy as jnp
import numpy as np
from jax import lax
from jax.experimental import pallas as pl
from jax.experimental.pallas import tpu as pltpu
from jax.sharding import PartitionSpec as P

HEAD_SIZE = 128
SEQUENCE_LENGTH = 384
epsilon = 1e-06
rope_base = 1000000.0
F32 = jnp.float32
BF16 = jnp.bfloat16
VMEM_BYTES = 56 * 1024 * 1024


def dot_nn(a, b):
    return lax.dot_general(a, b, (((1,), (0,)), ((), ())), preferred_element_type=F32)


def dot_nt(a, b):
    return lax.dot_general(a, b, (((1,), (1,)), ((), ())), preferred_element_type=F32)


def dot_tn(a, b):
    return lax.dot_general(a, b, (((0,), (0,)), ((), ())), preferred_element_type=F32)


def rope_tables():
    half = HEAD_SIZE // 2
    frequency = rope_base ** (-np.arange(half, dtype=np.float64) * (2.0 / HEAD_SIZE))
    angle = np.arange(SEQUENCE_LENGTH, dtype=np.float64)[:, None] * frequency[None, :]
    cosine, sine = np.cos(angle), np.sin(angle)
    return (
        np.concatenate([cosine, cosine], 1).astype(np.float32),
        np.concatenate([-sine, sine], 1).astype(np.float32),
    )


def inv_rms(v):
    return lax.rsqrt(jnp.mean(v * v, -1, keepdims=True) + epsilon)


def params(n):
    return pltpu.CompilerParams(
        dimension_semantics=("arbitrary",) * n, vmem_limit_bytes=VMEM_BYTES
    )


def whole(shape):
    return pl.BlockSpec(shape, lambda *g: (0,) * len(shape))


def attn_fwd_kernel(
    x_ref, gain_ref, wq_ref, wk_ref, wv_ref, wo_ref, qg_ref, kg_ref, cos_ref, sin_ref,
    n1_ref, qraw_ref, kraw_ref, qrot_ref, krot_ref, v_ref, p_ref, al_ref, branch_ref, blow_ref,
):
    g = pl.program_id(0)
    rows = x_ref.shape[0]
    heads = wq_ref.shape[1] // HEAD_SIZE

    @pl.when(g == 0)
    def _():
        x = x_ref[...].astype(F32)
        n1_ref[...] = (x * inv_rms(x) * gain_ref[...]).astype(BF16)
        branch_ref[...] = jnp.zeros_like(branch_ref)

    n1 = n1_ref[...]
    q_raw = dot_nn(n1, wq_ref[...])
    kv = dot_nn(n1, jnp.concatenate([wk_ref[...], wv_ref[...]], 1))
    k_raw = kv[:, :HEAD_SIZE]
    v = kv[:, HEAD_SIZE:].astype(BF16)
    qraw_ref[...] = q_raw
    kraw_ref[...] = k_raw
    v_ref[...] = v
    cosine, sine = cos_ref[...], sin_ref[...]

    def rotate(raw, gain):
        n = raw * inv_rms(raw) * gain
        return n * cosine + pltpu.roll(n, HEAD_SIZE // 2, 1) * sine

    scale = HEAD_SIZE ** (-0.5)
    k_rot = rotate(k_raw, kg_ref[...]).astype(BF16)
    krot_ref[...] = k_rot
    q_rot = jnp.concatenate(
        [
            (rotate(q_raw[:, h * HEAD_SIZE : (h + 1) * HEAD_SIZE], qg_ref[...]) * scale).astype(BF16)
            for h in range(heads)
        ],
        0,
    )
    qrot_ref[...] = q_rot[None]
    scores = dot_nt(q_rot, k_rot)
    q_pos = lax.broadcasted_iota(jnp.int32, (heads * rows, rows), 0)
    for _ in range(heads - 1):
        q_pos = jnp.where(q_pos >= rows, q_pos - rows, q_pos)
    k_pos = lax.broadcasted_iota(jnp.int32, (heads * rows, rows), 1)
    scores = jnp.where(k_pos <= q_pos, scores, -1e30)
    raised = jnp.exp(scores - jnp.max(scores, -1, keepdims=True))
    prob = (raised * (1.0 / jnp.sum(raised, -1, keepdims=True))).astype(BF16)
    p_ref[...] = prob[None]
    mixed = dot_nn(prob, v).astype(BF16)
    attn_low = jnp.concatenate([mixed[h * rows : (h + 1) * rows] for h in range(heads)], 1)
    al_ref[...] = attn_low
    branch_ref[...] += dot_nn(attn_low, wo_ref[...])

    @pl.when(g == pl.num_programs(0) - 1)
    def _():
        blow_ref[...] = branch_ref[...].astype(BF16)


def attn_fwd(x, attn_gain, wq, wk, wv, wo, q_gain, k_gain, cosine, sine):
    rows, width = x.shape
    groups = wk.shape[1] // HEAD_SIZE
    heads = wq.shape[1] // wk.shape[1]
    qw = heads * HEAD_SIZE
    col = lambda n: pl.BlockSpec((rows, n), lambda g: (0, g))
    wcol = lambda n: pl.BlockSpec((width, n), lambda g: (0, g))
    sds = jax.ShapeDtypeStruct
    return pl.pallas_call(
        attn_fwd_kernel,
        grid=(groups,),
        in_specs=[
            whole((rows, width)), whole((1, width)), wcol(qw), wcol(HEAD_SIZE), wcol(HEAD_SIZE),
            pl.BlockSpec((qw, width), lambda g: (g, 0)),
            whole((1, HEAD_SIZE)), whole((1, HEAD_SIZE)), whole((rows, HEAD_SIZE)), whole((rows, HEAD_SIZE)),
        ],
        out_specs=[
            whole((rows, width)), col(qw), col(HEAD_SIZE),
            pl.BlockSpec((1, heads * rows, HEAD_SIZE), lambda g: (g, 0, 0)),
            col(HEAD_SIZE), col(HEAD_SIZE),
            pl.BlockSpec((1, heads * rows, rows), lambda g: (g, 0, 0)),
            col(qw), whole((rows, width)), whole((rows, width)),
        ],
        out_shape=[
            sds((rows, width), BF16), sds((rows, groups * qw), F32), sds((rows, groups * HEAD_SIZE), F32),
            sds((groups, heads * rows, HEAD_SIZE), BF16),
            sds((rows, groups * HEAD_SIZE), BF16), sds((rows, groups * HEAD_SIZE), BF16),
            sds((groups, heads * rows, rows), BF16),
            sds((rows, groups * qw), BF16), sds((rows, width), F32), sds((rows, width), BF16),
        ],
        compiler_params=params(1),
        name="attention_forward",
    )(x, attn_gain, wq, wk, wv, wo, q_gain, k_gain, cosine, sine)


def mlp_kernel(
    x_ref, own_ref, other_ref, gain_ref, cot_ref, wg_ref, wu_ref, wd_ref,
    mid_ref, n2_ref, hid_ref, gg_ref, ug_ref, out_ref, ngrad_ref, acc_out, acc_n,
):
    j = pl.program_id(0)

    @pl.when(j == 0)
    def _():
        middle = x_ref[...].astype(F32) + (own_ref[...] + other_ref[...].astype(F32))
        mid_ref[...] = middle
        n2_ref[...] = (middle * inv_rms(middle) * gain_ref[...]).astype(BF16)
        acc_out[...] = jnp.zeros_like(acc_out)
        acc_n[...] = jnp.zeros_like(acc_n)

    n2 = n2_ref[...]
    wg, wu, wd = wg_ref[...], wu_ref[...], wd_ref[...]
    gate = dot_nn(n2, wg)
    up = dot_nn(n2, wu)
    sig = jax.nn.sigmoid(gate)
    silu = gate * sig
    hidden = (silu * up).astype(BF16)
    hid_ref[...] = hidden
    acc_out[...] += dot_nn(hidden, wd)
    hgrad = dot_nt(cot_ref[...], wd)
    ggrad = (hgrad * up * sig * (1.0 + gate * (1.0 - sig))).astype(BF16)
    ugrad = (hgrad * silu).astype(BF16)
    gg_ref[...] = ggrad
    ug_ref[...] = ugrad
    acc_n[...] += dot_nt(ggrad, wg) + dot_nt(ugrad, wu)

    @pl.when(j == pl.num_programs(0) - 1)
    def _():
        out_ref[...] = acc_out[...].astype(BF16)
        ngrad_ref[...] = acc_n[...].astype(BF16)


def mlp(x, own, other, gain, cot, wg, wu, wd):
    rows, width = x.shape
    units = wg.shape[1]
    step = 256 if units % 256 == 0 else 128
    full = whole((rows, width))
    col = pl.BlockSpec((rows, step), lambda j: (0, j))
    wcol = pl.BlockSpec((width, step), lambda j: (0, j))
    sds = jax.ShapeDtypeStruct
    return pl.pallas_call(
        mlp_kernel,
        grid=(units // step,),
        in_specs=[full, full, full, whole((1, width)), full, wcol, wcol,
                  pl.BlockSpec((step, width), lambda j: (j, 0))],
        out_specs=[full, full, col, col, col, full, full],
        out_shape=[
            sds((rows, width), F32), sds((rows, width), BF16),
            sds((rows, units), BF16), sds((rows, units), BF16), sds((rows, units), BF16),
            sds((rows, width), BF16), sds((rows, width), BF16),
        ],
        scratch_shapes=[pltpu.VMEM((rows, width), F32), pltpu.VMEM((rows, width), F32)],
        compiler_params=params(1),
        name="feed_forward",
    )(x, own, other, gain, cot, wg, wu, wd)


def wgrad_kernel(a_ref, b_ref, o_ref):
    o_ref[...] = dot_tn(a_ref[...], b_ref[...]).astype(BF16)


def wgrad(a, b, name):
    rows, m = a.shape
    n = b.shape[1]
    step = 256 if m % 256 == 0 else 128
    return pl.pallas_call(
        wgrad_kernel,
        grid=(m // step,),
        in_specs=[pl.BlockSpec((rows, step), lambda j: (0, j)), whole((rows, n))],
        out_specs=pl.BlockSpec((step, n), lambda j: (j, 0)),
        out_shape=jax.ShapeDtypeStruct((m, n), BF16),
        compiler_params=params(1),
        name=name,
    )(a, b)


def attn_bwd_kernel(
    nown_ref, nother_ref, mid_ref, cot_ref, mgain_ref, n1_ref, al_ref, p_ref, qraw_ref, kraw_ref, qrot_ref,
    krot_ref, v_ref, wq_ref, wk_ref, wv_ref, wo_ref, qg_ref, kg_ref, cos_ref, sin_ref,
    mgrad_ref, mgg_ref, owg_ref, qwg_ref, kwg_ref, vwg_ref, qgg_ref, kgg_ref, n1g_ref, blow, acc,
):
    g = pl.program_id(0)
    rows = mid_ref.shape[0]
    heads = wq_ref.shape[1] // HEAD_SIZE

    @pl.when(g == 0)
    def _():
        ngrad = nown_ref[...].astype(F32) + nother_ref[...].astype(F32)
        middle = mid_ref[...]
        inv = inv_rms(middle)
        u = middle * inv
        mgg_ref[...] = jnp.sum(ngrad * u, 0, keepdims=True)
        s = ngrad * mgain_ref[...]
        mgrad = cot_ref[...].astype(F32) + inv * (s - u * jnp.mean(s * u, -1, keepdims=True))
        mgrad_ref[...] = mgrad
        blow[...] = mgrad.astype(BF16)
        acc[...] = jnp.zeros_like(acc)
        qgg_ref[...] = jnp.zeros_like(qgg_ref)
        kgg_ref[...] = jnp.zeros_like(kgg_ref)

    branch_low = blow[...]
    agrad = dot_nt(branch_low, wo_ref[...]).astype(BF16)
    owg_ref[...] = dot_tn(al_ref[...], branch_low).astype(BF16)
    agrad = jnp.concatenate([agrad[:, h * HEAD_SIZE : (h + 1) * HEAD_SIZE] for h in range(heads)], 0)
    prob = p_ref[0]
    pgrad = dot_nt(agrad, v_ref[...])
    prob_wide = prob.astype(F32)
    row_dot = jnp.sum(pgrad * prob_wide, -1, keepdims=True)
    sgrad = (prob_wide * (pgrad - row_dot)).astype(BF16)
    vgrad = dot_tn(prob, agrad).astype(BF16)
    qrgrad = dot_nn(sgrad, krot_ref[...])
    krgrad = dot_tn(sgrad, qrot_ref[0])
    cosine, sine = cos_ref[...], sin_ref[...]

    def back(raw, gain, grad):
        inv = inv_rms(raw)
        u = raw * inv
        dn = grad * cosine + pltpu.roll(grad * sine, HEAD_SIZE // 2, 1)
        s = dn * gain
        return (
            (inv * (s - u * jnp.mean(s * u, -1, keepdims=True))).astype(BF16),
            jnp.sum(dn * u, 0, keepdims=True),
        )

    scale = HEAD_SIZE ** (-0.5)
    grads = []
    q_raw = qraw_ref[...]
    for h in range(heads):
        qgrad, qgg = back(
            q_raw[:, h * HEAD_SIZE : (h + 1) * HEAD_SIZE], qg_ref[...], qrgrad[h * rows : (h + 1) * rows] * scale
        )
        qgg_ref[...] += qgg
        grads.append(qgrad)
    kgrad, kgg = back(kraw_ref[...], kg_ref[...], krgrad)
    kgg_ref[...] += kgg
    grads += [kgrad, vgrad]
    grads = jnp.concatenate(grads, 1)
    wg = dot_tn(n1_ref[...], grads).astype(BF16)
    qw = heads * HEAD_SIZE
    qwg_ref[...] = wg[:, :qw]
    kwg_ref[...] = wg[:, qw : qw + HEAD_SIZE]
    vwg_ref[...] = wg[:, qw + HEAD_SIZE :]
    acc[...] += dot_nt(grads, jnp.concatenate([wq_ref[...], wk_ref[...], wv_ref[...]], 1))

    @pl.when(g == pl.num_programs(0) - 1)
    def _():
        n1g_ref[...] = acc[...].astype(BF16)


def attn_bwd(nown, nother, middle, cot, mgain, n1, al, prob, qraw, kraw, qrot, krot, v, wq, wk, wv, wo, qg, kg,
             cosine, sine):
    rows, width = middle.shape
    groups = wk.shape[1] // HEAD_SIZE
    heads = wq.shape[1] // wk.shape[1]
    qw = heads * HEAD_SIZE
    full = whole((rows, width))
    col = lambda n: pl.BlockSpec((rows, n), lambda g: (0, g))
    wcol = lambda n: pl.BlockSpec((width, n), lambda g: (0, g))
    wrow = pl.BlockSpec((qw, width), lambda g: (g, 0))
    stack = lambda n: pl.BlockSpec((1, heads * rows, n), lambda g: (g, 0, 0))
    sds = jax.ShapeDtypeStruct
    return pl.pallas_call(
        attn_bwd_kernel,
        grid=(groups,),
        in_specs=[
            full, full, full, full, whole((1, width)), full, col(qw), stack(rows), col(qw), col(HEAD_SIZE),
            stack(HEAD_SIZE), col(HEAD_SIZE), col(HEAD_SIZE), wcol(qw), wcol(HEAD_SIZE), wcol(HEAD_SIZE), wrow,
            whole((1, HEAD_SIZE)), whole((1, HEAD_SIZE)), whole((rows, HEAD_SIZE)), whole((rows, HEAD_SIZE)),
        ],
        out_specs=[
            full, whole((1, width)), wrow, wcol(qw), wcol(HEAD_SIZE), wcol(HEAD_SIZE),
            whole((1, HEAD_SIZE)), whole((1, HEAD_SIZE)), full,
        ],
        out_shape=[
            sds((rows, width), F32), sds((1, width), F32), sds((groups * qw, width), BF16),
            sds((width, groups * qw), BF16), sds((width, groups * HEAD_SIZE), BF16),
            sds((width, groups * HEAD_SIZE), BF16),
            sds((1, HEAD_SIZE), F32), sds((1, HEAD_SIZE), F32), sds((rows, width), BF16),
        ],
        scratch_shapes=[pltpu.VMEM((rows, width), BF16), pltpu.VMEM((rows, width), F32)],
        compiler_params=params(1),
        name="attention_backward",
    )(nown, nother, middle, cot, mgain, n1, al, prob, qraw, kraw, qrot, krot, v, wq, wk, wv, wo, qg, kg,
      cosine, sine)


def swap(x, axis, n, bit):
    return lax.ppermute(x, axis, [(i, i ^ bit) for i in range(n)])


def line_hops(n, stride):
    length = n // stride
    shift = lambda a, b: [(a * stride + r, b * stride + r) for r in range(stride)]
    last = length - 1
    inward = [shift(s, s + 1) + shift(last - s, last - s - 1) for s in range(length // 2 - 1)]
    middle = length // 2
    across = shift(middle - 1, middle) + shift(middle, middle - 1)
    outward = [shift(s + 1, s) + shift(last - s - 1, last - s) for s in reversed(range(length // 2 - 1))]
    return inward, across, outward


def add(a, b):
    return (a.astype(F32) + b.astype(F32)).astype(BF16)


def half_of(x, bit, axis=0):
    size = x.shape[axis] // 2
    return lax.dynamic_slice_in_dim(x, bit * size, size, axis)


def join(bit, own, other):
    return jnp.where(bit == 0, jnp.concatenate([own, other], 0), jnp.concatenate([other, own], 0))


def sum_over_dp(x, n):
    place = lax.axis_index("dp")
    core, pair, spot = place % 2, (place // 2) % 2, place // 4
    x = add(half_of(x, core), swap(half_of(x, 1 - core), "dp", n, 1))
    x = add(half_of(x, pair), swap(half_of(x, 1 - pair), "dp", n, 2))
    inward, across, outward = line_hops(n, 4)
    for hop in inward:
        x = add(x, lax.ppermute(x, "dp", hop))
    x = add(x, lax.ppermute(x, "dp", across))
    for step, hop in enumerate(outward):
        edge = len(outward) - 1 - step
        takes = (spot == edge) | (spot == n // 4 - 1 - edge)
        x = jnp.where(takes, lax.ppermute(x, "dp", hop), x)
    beside = swap(x, "dp", n, 2)
    far, far_beside = swap(x, "dp", n, 1), swap(beside, "dp", n, 1)
    return join(core, join(pair, x, beside), join(pair, far, far_beside)).astype(F32)


def sum_small(x, n, tensor):
    x = x + swap(x, "dp", n, 1)
    x = x + swap(x, "dp", n, 2)
    inward, across, outward = line_hops(n, 4)
    spot = lax.axis_index("dp") // 4
    for hop in inward:
        x = x + lax.ppermute(x, "dp", hop)
    x = x + lax.ppermute(x, "dp", across)
    for step, hop in enumerate(outward):
        edge = len(outward) - 1 - step
        takes = (spot == edge) | (spot == n // 4 - 1 - edge)
        x = jnp.where(takes, lax.ppermute(x, "dp", hop), x)
    return x + swap(x, "tensor", 2, 1) if tensor == 2 else lax.psum(x, "tensor")


def others(x, tensor):
    if tensor == 2:
        return swap(x, "tensor", 2, 1)
    return (lax.psum(x.astype(F32), "tensor") - x.astype(F32)).astype(x.dtype)


def features(x, tensor):
    if tensor == 2:
        other = swap(x, "tensor", 2, 1)
        first = lax.axis_index("tensor") == 0
        return jnp.where(first, jnp.concatenate([x, other], 1), jnp.concatenate([other, x], 1))
    return lax.all_gather(x, "tensor", axis=1, tiled=True)


def per_device(
    dp, tensor, tokens, cotangent, attn_gain, query_weight, key_matrix, value_matrix, query_gain,
    key_norm_gain, out_weight, mlp_gain, gate_weight, up_weight, down_weight,
):
    x = features(tokens, tensor)
    cot = features(cotangent, tensor)
    rows, width = x.shape
    share = tokens.shape[1]
    offset = lax.axis_index("tensor") * share
    mine = lambda a: lax.dynamic_slice_in_dim(a, offset, share, 1)
    cosine, sine = (jnp.asarray(t) for t in rope_tables())
    attn_gain, mlp_gain = attn_gain[None], mlp_gain[None]
    query_gain, key_norm_gain = query_gain[None], key_norm_gain[None]

    n1, qraw, kraw, qrot, krot, v, prob, al, branch, branch_low = attn_fwd(
        x, attn_gain, query_weight, key_matrix, value_matrix, out_weight, query_gain, key_norm_gain, cosine, sine
    )
    middle, n2, hidden, ggrad, ugrad, mlp_part, ngrad = mlp(
        x, branch, others(branch_low, tensor), mlp_gain, cot, gate_weight, up_weight, down_weight
    )
    ngrad_other = others(ngrad, tensor)
    down_wgrad = sum_over_dp(wgrad(hidden, cot, "down_gradient"), dp)
    gate_wgrad = sum_over_dp(wgrad(n2, ggrad, "gate_gradient"), dp)
    up_wgrad = sum_over_dp(wgrad(n2, ugrad, "up_gradient"), dp)
    mgrad, mgg, owg, qwg, kwg, vwg, qgg, kgg, n1g = attn_bwd(
        ngrad, ngrad_other, middle, cot, mlp_gain, n1, al, prob, qraw, kraw, qrot, krot, v,
        query_weight, key_matrix, value_matrix, out_weight, query_gain, key_norm_gain, cosine, sine,
    )
    out_wgrad = sum_over_dp(owg, dp)
    query_wgrad = sum_over_dp(qwg, dp)
    kv_wgrad = sum_over_dp(jnp.concatenate([kwg, vwg], 1), dp)
    key_wgrad, value_wgrad = kv_wgrad[:, : kwg.shape[1]], kv_wgrad[:, kwg.shape[1] :]

    if tensor == 2:
        t = lax.axis_index("tensor")
        arrived = swap(half_of(mlp_part, 1 - t, 1), "tensor", 2, 1)
        mlp_share = mine(mlp_part).astype(F32) + arrived.astype(F32)
    else:
        mlp_share = lax.psum_scatter(mlp_part, "tensor", scatter_dimension=1, tiled=True).astype(F32)
    layer_out = (mine(middle) + mlp_share).astype(BF16)

    n1_grad = n1g.astype(F32) + others(n1g, tensor).astype(F32)
    wide = x.astype(F32)
    inv_one = inv_rms(wide)
    u = wide * inv_one
    s = n1_grad * attn_gain
    mean = jnp.mean(s * u, -1, keepdims=True)
    input_grad = (mine(mgrad) + inv_one * (mine(s) - mine(u) * mean)).astype(BF16)
    agg = jnp.sum(n1_grad * u, 0, keepdims=True)

    here = jnp.arange(width)[None] // share == lax.axis_index("tensor")
    small = jnp.concatenate([jnp.where(here, agg, 0.0), jnp.where(here, mgg, 0.0), qgg, kgg], 1)
    small = sum_small(small, dp, tensor)[0]
    return (
        layer_out, input_grad, small[:width], query_wgrad, key_wgrad, value_wgrad,
        small[2 * width : 2 * width + HEAD_SIZE], small[2 * width + HEAD_SIZE :], out_wgrad,
        small[width : 2 * width], gate_wgrad, up_wgrad, down_wgrad,
    )


def solution(mesh):
    rows, cols, rep = P("tensor", None), P(None, "tensor"), P()
    both = P("dp", "tensor")
    return jax.shard_map(
        functools.partial(per_device, mesh.shape["dp"], mesh.shape["tensor"]),
        mesh=mesh,
        in_specs=(both, both, rep, cols, cols, cols, rep, rep, rows, rep, cols, cols, rows),
        out_specs=(both, both, rep, cols, cols, cols, rep, rep, rows, rep, cols, cols, rows),
        check_vma=False,
    )
```

time: 578 us -> 520 us (0.90)
  blocking collectives: 85.3 us -> 0 us
  Pallas kernels: 0 us -> 74.6 us
  starting transfers between devices: 0.42 us -> 62.6 us
  matrix products: 61.6 us -> 0 us
  other arithmetic: 66.2 us -> 36.1 us
  local copies, waits for them, and re-layouts: 34.8 us -> 17.1 us
  between operations: 15.1 us -> 1.8 us
  waiting for transfers between devices: 305 us -> 318 us
    ppermute x0 -> x60, waiting for transfers between devices: none -> 318 us  [the longest x39 169 us: swap(): return lax.ppermute(x, axis, [(i, i ^ bit) for i in range(n)])]
    psum x1 -> x0, waiting for transfers between devices: 246 us -> none  [per_device(): lax.psum(query_wgrad.astype(jnp.bfloat16), 'dp').astype(jnp.float32)]
    pallas_call x0 -> x6, Pallas kernels: none -> 74.6 us  [the longest x1 22.5 us: attn_bwd(): pl.pallas_call(attn_bwd_kernel, grid=(groups,), in_specs=[full, full, ful...]
    ppermute x0 -> x60, starting transfers between devices: none -> 62.6 us  [the longest x39 29.4 us: swap(): return lax.ppermute(x, axis, [(i, i ^ bit) for i in range(n)])]
    dot_general x27 -> x0, matrix products: 61.6 us -> none  [the longest x7 22.8 us: dot_rows(): lax.dot_general(left, right, (((0,), (0,)), ((), ())), preferred_element_...]
    psum x3 -> x0, blocking collectives: 45.9 us -> none  [the longest x1 32.5 us: per_device(): lax.psum(attn_gain_grad.astype(jnp.bfloat16), 'dp').astype(jnp.float32)]
    reduce_scatter x4 -> x0, waiting for transfers between devices: 45.4 us -> none  [the longest x1 27.6 us: per_device(): lax.psum_scatter(branch_part, 'tensor', scatter_dimension=1, tiled=True)]
    all_gather x3 -> x0, blocking collectives: 39.5 us -> none  [the longest x1 15.7 us: per_device(): lax.all_gather(cotangent, 'tensor', axis=1, tiled=True)]
  transfers between devices with their start and end apart: 6 -> 60, of which waited for: 4 -> 24; matrix products, arithmetic and copies ran while one was open for 8% -> 8% of each run, Pallas kernels for 0% -> 8%
where the time goes in v1:
time: 520 us; the launch traced here: 510 us
  waiting for transfers between devices  318 us (61%)
  Pallas kernels  74.6 us (14%)
  starting transfers between devices  62.6 us (12%)
  other arithmetic  36.1 us (7%)
  local copies, waits for them, and re-layouts  17.1 us (3%)
    ppermute x39, waiting for transfers between devices, swap(): return lax.ppermute(x, axis, [(i, i ^ bit) for i in range(n)])  169 us
    ppermute x6, waiting for transfers between devices, sum_over_dp(): x = jnp.where(takes, lax.ppermute(x, 'dp', hop), x)  75.3 us
    ppermute x6, waiting for transfers between devices, sum_over_dp(): x = add(x, lax.ppermute(x, 'dp', hop))  64.3 us
    ppermute x39, starting transfers between devices, swap(): return lax.ppermute(x, axis, [(i, i ^ bit) for i in range(n)])  29.4 us
    pallas_call x1, Pallas kernels, attn_bwd(): pl.pallas_call(attn_bwd_kernel, grid=(groups,), in_specs=[full, full, ful...  22.5 us
    pallas_call x1, Pallas kernels, mlp(): pl.pallas_call(mlp_kernel, grid=(units // step,), in_specs=[full, full, f...  19.9 us
    pallas_call x3, Pallas kernels, wgrad(): pl.pallas_call(wgrad_kernel, grid=(m // step,), in_specs=[pl.BlockSpec((r...  16.9 us
    convert_element_type x6, other arithmetic, sum_over_dp(): join(core, join(pair, x, beside), join(pair, far, far_beside)).astype(F32)  16.3 us
  transfers between devices with their start and end apart: 60, of which 24 were waited for; matrix products, arithmetic and copies ran while one was open for 8% of the time, Pallas kernels for 8%

profile of v1, /device:TPU:0, one launch (start us, length us, event | category | flops | bytes accessed | tf_op | source)
XLA Modules:
  0.0 510.3 jit_solution(1483615803967699699)
XLA Ops:
  0.6 3.0 collective-permute-start
  3.7 9.3 %collective-permute-done = bf16[384,512]{1,0:T(8,128)(2,1)S(1)} collective-permute-done((bf16[384,512]{1,0:T(8,128)(2,1)}, bf16[384,512]{1,0:T(8,128)(2,1)S(1)}, u32[]{:S(2)}, u32[]{:S(2)}) %collective-permute-start) | collective-permute-done | bytes 393248 | tf_op jit(solution)/shard_map/ppermute | solution.py:341
  13.0 2.3 fusion.6
  15.3 15.4 %attention_forward.1 = (bf16[384,1024]{1,0:T(8,128)(2,1)}, f32[384,1024]{1,0:T(8,128)}, f32[384,512]{1,0:T(8,128)}, bf16[4,768,128]{2,1,0:T(8,128)(2,1)}, bf16[3...) custom-call(bf16[384,1024]{1,0:T(8,128)(2,1)} %get-tuple-element.69., ...), custom_call_target="tpu_custom_call" | custom-call | tf_op jit(solution)/shard_map/attention_forward/pallas_call | solution.py:123
  30.7 1.8 collective-permute-start.1
  32.8 25.3 %collective-permute-done.2 = bf16[384,512]{1,0:T(8,128)(2,1)S(1)} collective-permute-done((bf16[384,512]{1,0:T(8,128)(2,1)S(1)}, bf16[384,512]{1,0:T(8,128)(2,1)S(1)}, u32[]{:S(2)}, u32[]{:S(2)}) %collective-permute-start.2) | collective-permute-done | bytes 393248 | tf_op jit(solution)/shard_map/ppermute | solution.py:341
  60.1 19.9 %feed_forward.1 = (f32[384,1024]{1,0:T(8,128)}, bf16[384,1024]{1,0:T(8,128)(2,1)}, bf16[384,1536]{1,0:T(8,128)(2,1)}, bf16[384,1536]{1,0:T(8,128)(2,1)}, bf16[38...) custom-call(bf16[384,1024]{1,0:T(8,128)(2,1)} %get-tuple-element.69.x_ref, ...), custom_call_target="tpu_custom_call" | custom-call | tf_op jit(solution)/shard_map/feed_forward/pallas_call | solution.py:194
  80.0 1.8 constant_dynamic-slice_fusion.12
  81.8 1.4 collective-permute-start.3
  83.8 6.3 %down_gradient.1 = bf16[1536,1024]{1,0:T(8,128)(2,1)} custom-call(bf16[384,1536]{1,0:T(8,128)(2,1)} %get-tuple-element.64.a_ref, bf16[384,1024]{1,0:T(8,128)(2,1)} %maximum_select_fusion.19.cot_ref.b_ref), custom_call_target="tpu_custom_call" | custom-call | tf_op jit(solution)/shard_map/down_gradient/pallas_call | solution.py:219
  90.1 2.7 constant_dynamic-slice_fusion
  92.8 5.3 %gate_gradient.1 = bf16[1024,1536]{1,0:T(8,128)(2,1)} custom-call(bf16[384,1024]{1,0:T(8,128)(2,1)} %get-tuple-element.61.a_ref, bf16[384,1536]{1,0:T(8,128)(2,1)} %get-tuple-element.62.b_ref), custom_call_target="tpu_custom_call" | custom-call | tf_op jit(solution)/shard_map/gate_gradient/pallas_call | solution.py:219
  98.1 2.7 constant_dynamic-slice_fusion.4
  100.8 5.3 %up_gradient.1 = bf16[1024,1536]{1,0:T(8,128)(2,1)} custom-call(bf16[384,1024]{1,0:T(8,128)(2,1)} %get-tuple-element.61.a_ref, bf16[384,1536]{1,0:T(8,128)(2,1)} %get-tuple-element.63.b_ref), custom_call_target="tpu_custom_call" | custom-call | tf_op jit(solution)/shard_map/up_gradient/pallas_call | solution.py:219
  106.6 1.7 constant_dynamic-slice_fusion.2
  109.3 22.5 %attention_backward.1 = (f32[384,1024]{1,0:T(8,128)}, f32[1,1024]{1,0:T(1,128)}, bf16[1024,1024]{1,0:T(8,128)(2,1)}, bf16[1024,1024]{1,0:T(8,128)(2,1)}, bf16[10...) custom-call(bf16[384,1024]{1,0:T(8,128)(2,1)} %get-tuple-element.43., ...), custom_call_target="tpu_custom_call" | custom-call | tf_op jit(solution)/shard_map/attention_backward/pallas_call | solution.py:315
  131.8 1.5 collective-permute-start.5
  133.3 1.4 constant_dynamic-slice_fusion.10
  136.3 15.7 %collective-permute-done.5 = bf16[384,1024]{1,0:T(8,128)(2,1)S(1)} collective-permute-done((bf16[384,1024]{1,0:T(8,128)(2,1)}, bf16[384,1024]{1,0:T(8,128)(2,1)S(1)}, u32[]{:S(2)}, u32[]{:S(2)}) %collective-permute-start.5) | collective-permute-done | bytes 786464 | tf_op jit(solution)/shard_map/ppermute | solution.py:341
  156.2 1.5 collective-permute-start.7
  157.7 2.3 collective-permute-done.7
  159.9 3.4 collective-permute-start.8
  164.7 1.5 collective-permute-start.53
  167.5 1.3 collective-permute-start.10
  168.8 8.3 %collective-permute-done.10 = f32[1,2304]{1,0:T(1,128)S(1)} collective-permute-done((f32[1,2304]{1,0:T(1,128)S(1)}, f32[1,2304]{1,0:T(1,128)S(1)}, u32[]{:S(2)}, u32[]{:S(2)}) %collective-permute-start.10) | collective-permute-done | bytes 9248 | tf_op jit(solution)/shard_map/ppermute | solution.py:397
  177.1 1.6 collective-permute-start.11
  182.5 1.5 collective-permute-start.45
  185.6 1.6 collective-permute-start.13
  187.6 42.5 %collective-permute-done.29 = bf16[256,1024]{1,0:T(8,128)(2,1)S(1)} collective-permute-done((bf16[256,1024]{1,0:T(8,128)(2,1)S(1)}, bf16[256,1024]{1,0:T(8,128)(2,1)S(1)}, u32[]{:S(2)}, u32[]{:S(2)}) %collective-permute-start.29) | collective-permute-done | bytes 524320 | tf_op jit(solution)/shard_map/ppermute | solution.py:341
  230.1 1.5 collective-permute-start.21
  231.8 9.5 %collective-permute-done.13 = bf16[256,1024]{1,0:T(8,128)(2,1)S(1)} collective-permute-done((bf16[256,1024]{1,0:T(8,128)(2,1)S(1)}, bf16[256,1024]{1,0:T(8,128)(2,1)S(1)}, u32[]{:S(2)}, u32[]{:S(2)}) %collective-permute-start.13) | collective-permute-done | bytes 524320 | tf_op jit(solution)/shard_map/ppermute | solution.py:341
  241.4 4.2 collective-permute-start.30
  245.8 1.3 collective-permute-start.14
  247.4 1.3 collective-permute-start.54
  249.0 1.3 collective-permute-start.38
  250.6 3.0 collective-permute-start.46
  253.8 4.1 collective-permute-done.30
  257.9 4.4 collective-permute-start.22
  262.5 6.6 %collective-permute-done.14 = bf16[256,1024]{1,0:T(8,128)(2,1)S(1)} collective-permute-done((bf16[256,1024]{1,0:T(8,128)(2,1)S(1)}, bf16[256,1024]{1,0:T(8,128)(2,1)S(1)}, u32[]{:S(2)}, u32[]{:S(2)}) %collective-permute-start.14) | collective-permute-done | bytes 524320 | tf_op jit(solution)/shard_map/ppermute | solution.py:375
  270.0 53.6 %collective-permute-done.22 = bf16[256,1024]{1,0:T(8,128)(2,1)S(1)} collective-permute-done((bf16[256,1024]{1,0:T(8,128)(2,1)S(1)}, bf16[256,1024]{1,0:T(8,128)(2,1)S(1)}, u32[]{:S(2)}, u32[]{:S(2)}) %collective-permute-start.22) | collective-permute-done | bytes 524320 | tf_op jit(solution)/shard_map/ppermute | solution.py:375
  328.3 1.3 collective-permute-start.32
  329.8 1.3 collective-permute-start.16
  331.3 25.6 %collective-permute-done.32 = bf16[256,1024]{1,0:T(8,128)(2,1)S(1)} collective-permute-done((bf16[256,1024]{1,0:T(8,128)(2,1)S(1)}, bf16[256,1024]{1,0:T(8,128)(2,1)S(1)}, u32[]{:S(2)}, u32[]{:S(2)}) %collective-permute-start.32) | collective-permute-done | bytes 524320 | tf_op jit(solution)/shard_map/ppermute | solution.py:380
  358.3 5.7 %collective-permute-done.16 = bf16[256,1024]{1,0:T(8,128)(2,1)S(1)} collective-permute-done((bf16[256,1024]{1,0:T(8,128)(2,1)S(1)}, bf16[256,1024]{1,0:T(8,128)(2,1)S(1)}, u32[]{:S(2)}, u32[]{:S(2)}) %collective-permute-start.16) | collective-permute-done | bytes 524320 | tf_op jit(solution)/shard_map/ppermute | solution.py:380
  364.1 5.6 %collective-permute-done.24 = bf16[256,1024]{1,0:T(8,128)(2,1)S(1)} collective-permute-done((bf16[256,1024]{1,0:T(8,128)(2,1)S(1)}, bf16[256,1024]{1,0:T(8,128)(2,1)S(1)}, u32[]{:S(2)}, u32[]{:S(2)}) %collective-permute-start.24) | collective-permute-done | bytes 524320 | tf_op jit(solution)/shard_map/ppermute | solution.py:380
  369.7 1.5 collective-permute-start.33
  372.0 1.5 collective-permute-start.40
  373.7 1.6 collective-permute-start.25
  375.6 8.9 %collective-permute-done.33 = bf16[256,1024]{1,0:T(8,128)(2,1)S(1)} collective-permute-done((bf16[256,1024]{1,0:T(8,128)(2,1)S(1)}, bf16[256,1024]{1,0:T(8,128)(2,1)S(1)}, u32[]{:S(2)}, u32[]{:S(2)}) %collective-permute-start.33) | collective-permute-done | bytes 524320 | tf_op jit(solution)/shard_map/ppermute | solution.py:341
  385.0 10.4 %collective-permute-done.17 = bf16[256,1024]{1,0:T(8,128)(2,1)S(1)} collective-permute-done((bf16[256,1024]{1,0:T(8,128)(2,1)S(1)}, bf16[256,1024]{1,0:T(8,128)(2,1)S(1)}, u32[]{:S(2)}, u32[]{:S(2)}) %collective-permute-start.17) | collective-permute-done | bytes 524320 | tf_op jit(solution)/shard_map/ppermute | solution.py:341
  397.2 3.8 collective-permute-done.25
  401.5 10.5 %collective-permute-done.40 = bf16[256,1536]{1,0:T(8,128)(2,1)S(1)} collective-permute-done((bf16[256,1536]{1,0:T(8,128)(2,1)S(1)}, bf16[256,1536]{1,0:T(8,128)(2,1)S(1)}, u32[]{:S(2)}, u32[]{:S(2)}) %collective-permute-start.40) | collective-permute-done | bytes 786464 | tf_op jit(solution)/shard_map/ppermute | solution.py:380
  413.4 15.5 %collective-permute-done.48 = bf16[256,1536]{1,0:T(8,128)(2,1)S(1)} collective-permute-done((bf16[256,1536]{1,0:T(8,128)(2,1)S(1)}, bf16[256,1536]{1,0:T(8,128)(2,1)S(1)}, u32[]{:S(2)}, u32[]{:S(2)}) %collective-permute-start.48) | collective-permute-done | bytes 786464 | tf_op jit(solution)/shard_map/ppermute | solution.py:380
  428.9 12.4 %collective-permute-done.56 = bf16[384,1024]{1,0:T(8,128)(2,1)S(1)} collective-permute-done((bf16[384,1024]{1,0:T(8,128)(2,1)S(1)}, bf16[384,1024]{1,0:T(8,128)(2,1)S(1)}, u32[]{:S(2)}, u32[]{:S(2)}) %collective-permute-start.56) | collective-permute-done | bytes 786464 | tf_op jit(solution)/shard_map/ppermute | solution.py:380
  443.5 1.6 collective-permute-start.41
  446.1 2.5 fusion.9
  448.6 2.9 fusion.3
  451.4 1.5 collective-permute-start.57
  453.4 27.3 %collective-permute-done.49 = bf16[256,1536]{1,0:T(8,128)(2,1)S(1)} collective-permute-done((bf16[256,1536]{1,0:T(8,128)(2,1)S(1)}, bf16[256,1536]{1,0:T(8,128)(2,1)S(1)}, u32[]{:S(2)}, u32[]{:S(2)}) %collective-permute-start.49) | collective-permute-done | bytes 786464 | tf_op jit(solution)/shard_map/ppermute | solution.py:341
  480.8 2.9 fusion.5
  485.5 11.7 %collective-permute-done.57 = bf16[384,1024]{1,0:T(8,128)(2,1)S(1)} collective-permute-done((bf16[384,1024]{1,0:T(8,128)(2,1)S(1)}, bf16[384,1024]{1,0:T(8,128)(2,1)S(1)}, u32[]{:S(2)}, u32[]{:S(2)}) %collective-permute-start.57) | collective-permute-done | bytes 786464 | tf_op jit(solution)/shard_map/ppermute | solution.py:341
  499.0 3.1 fusion.1
  502.8 3.1 fusion
  506.6 3.5 fusion.2
  (180 shorter events, 41.4 us)
Async XLA Ops:
  0.6 12.4 %collective-permute-start = (bf16[384,512]{1,0:T(8,128)(2,1)}, bf16[384,512]{1,0:T(8,128)(2,1)S(1)}, u32[]{:S(2)}, u32[]{:S(2)}) collective-permute-start(bf16[384,512]{1,0:T(8,128)(2,1)} %param.15), channel_id=1, source_target_pairs={{0,1},{1,0},{2,3},{3,2},{4,5},{5,4},{6,7},{7,6},{8,9},{9,8},{10,11... | collective-permute-start | bytes 1179656 | tf_op jit(solution)/shard_map/ppermute | solution.py:341
  15.3 17.2 %copy-start.13 = (bf16[384,512]{1,0:T(8,128)(2,1)S(1)}, bf16[384,512]{1,0:T(8,128)(2,1)}, u32[]{:S(2)}) copy-start(bf16[384,512]{1,0:T(8,128)(2,1)} %param.16) | copy-start | bytes 1179652
  30.7 28.5 %collective-permute-start.1 = (bf16[384,1024]{1,0:T(8,128)(2,1)}, bf16[384,1024]{1,0:T(8,128)(2,1)S(1)}, u32[]{:S(2)}, u32[]{:S(2)}) collective-permute-start(bf16[384,1024]{1,0:T(8,128)(2,1)} %get-tuple-element.40), channel_id=1, source_target_pairs={{0,1},{1,0},{2,3},{3,2},{4,5},{5,4},{6,7},{7,6},{8,9},{9,8},{10,11... | collective-permute-start | bytes 2359304 | tf_op jit(solution)/shard_map/ppermute | solution.py:341
  32.5 25.6 %collective-permute-start.2 = (bf16[384,512]{1,0:T(8,128)(2,1)S(1)}, bf16[384,512]{1,0:T(8,128)(2,1)S(1)}, u32[]{:S(2)}, u32[]{:S(2)}) collective-permute-start(bf16[384,512]{1,0:T(8,128)(2,1)S(1)} %copy-done.13), channel_id=1, source_target_pairs={{0,1},{1,0},{2,3},{3,2},{4,5},{5,4},{6,7},{7,6},{8,9},{9,8},{10,11... | collective-permute-start | bytes 1179656 | tf_op jit(solution)/shard_map/ppermute | solution.py:341
  81.8 26.6 %collective-permute-start.3 = (bf16[384,512]{1,0:T(8,128)(2,1)}, bf16[384,512]{1,0:T(8,128)(2,1)S(1)}, u32[]{:S(2)}, u32[]{:S(2)}) collective-permute-start(bf16[384,512]{1,0:T(8,128)(2,1)} %constant_dynamic-slice_fusion.12), channel_id=1, source_target_pairs={{0,1},{1,0},{2,3},{3,2},{4,5},{5,4},{6,7},{7,6},{8,9},{9,8},{10,11... | collective-permute-start | bytes 1179656 | tf_op jit(solution)/shard_map/ppermute | solution.py:341
  83.2 26.1 %collective-permute-start.4 = (bf16[384,1024]{1,0:T(8,128)(2,1)}, bf16[384,1024]{1,0:T(8,128)(2,1)}, u32[]{:S(2)}, u32[]{:S(2)}) collective-permute-start(bf16[384,1024]{1,0:T(8,128)(2,1)} %get-tuple-element.43.nown_ref), channel_id=1, source_target_pairs={{0,1},{1,0},{2,3},{3,2},{4,5},{5,4},{6,7},{7,6},{8,9},{9,8},{10,11... | collective-permute-start | bytes 2359304 | tf_op jit(solution)/shard_map/ppermute | solution.py:341
  92.8 60.9 %collective-permute-start.52 = (bf16[768,1024]{1,0:T(8,128)(2,1)}, bf16[768,1024]{1,0:T(8,128)(2,1)S(1)}, u32[]{:S(2)}, u32[]{:S(2)}) collective-permute-start(bf16[768,1024]{1,0:T(8,128)(2,1)} %constant_dynamic-slice_fusion), channel_id=1, source_target_pairs={{0,2},{2,0},{4,6},{6,4},{8,10},{10,8},{12,14},{14,12},{16,18},{18,... | collective-permute-start | bytes 4718600 | tf_op jit(solution)/shard_map/ppermute | solution.py:341
  106.1 46.7 %collective-permute-start.36 = (bf16[512,1536]{1,0:T(8,128)(2,1)}, bf16[512,1536]{1,0:T(8,128)(2,1)S(1)}, u32[]{:S(2)}, u32[]{:S(2)}) collective-permute-start(bf16[512,1536]{1,0:T(8,128)(2,1)} %constant_dynamic-slice_fusion.4), channel_id=1, source_target_pairs={{0,2},{2,0},{4,6},{6,4},{8,10},{10,8},{12,14},{14,12},{16,18},{18,... | collective-permute-start | bytes 4718600 | tf_op jit(solution)/shard_map/ppermute | solution.py:341
  108.3 57.9 %collective-permute-start.44 = (bf16[512,1536]{1,0:T(8,128)(2,1)S(1)}, bf16[512,1536]{1,0:T(8,128)(2,1)S(1)}, u32[]{:S(2)}, u32[]{:S(2)}) collective-permute-start(bf16[512,1536]{1,0:T(8,128)(2,1)S(1)} %constant_dynamic-slice_fusion.2), channel_id=1, source_target_pairs={{0,2},{2,0},{4,6},{6,4},{8,10},{10,8},{12,14},{14,12},{16,18},{18,... | collective-permute-start | bytes 4718600 | tf_op jit(solution)/shard_map/ppermute | solution.py:341
  131.8 20.2 %collective-permute-start.5 = (bf16[384,1024]{1,0:T(8,128)(2,1)}, bf16[384,1024]{1,0:T(8,128)(2,1)S(1)}, u32[]{:S(2)}, u32[]{:S(2)}) collective-permute-start(bf16[384,1024]{1,0:T(8,128)(2,1)} %get-tuple-element.53), channel_id=1, source_target_pairs={{0,1},{1,0},{2,3},{3,2},{4,5},{5,4},{6,7},{7,6},{8,9},{9,8},{10,11... | collective-permute-start | bytes 2359304 | tf_op jit(solution)/shard_map/ppermute | solution.py:341
  134.8 47.7 %collective-permute-start.28 = (bf16[512,1024]{1,0:T(8,128)(2,1)S(1)}, bf16[512,1024]{1,0:T(8,128)(2,1)S(1)}, u32[]{:S(2)}, u32[]{:S(2)}) collective-permute-start(bf16[512,1024]{1,0:T(8,128)(2,1)S(1)} %constant_dynamic-slice_fusion.6), channel_id=1, source_target_pairs={{0,2},{2,0},{4,6},{6,4},{8,10},{10,8},{12,14},{14,12},{16,18},{18,... | collective-permute-start | bytes 3145736 | tf_op jit(solution)/shard_map/ppermute | solution.py:341
  136.2 16.5 %copy-start.16 = (f32[1,128]{1,0:T(1,128)S(1)}, f32[1,128]{1,0:T(1,128)}, u32[]{:S(2)}) copy-start(f32[1,128]{1,0:T(1,128)} %get-tuple-element.55) | copy-start | bytes 1540
  136.3 16.5 %copy-start.17 = (f32[1,128]{1,0:T(1,128)S(1)}, f32[1,128]{1,0:T(1,128)}, u32[]{:S(2)}) copy-start(f32[1,128]{1,0:T(1,128)} %get-tuple-element.56) | copy-start | bytes 1540
  136.3 17.1 %copy-start.3 = (bf16[1024,1536]{1,0:T(8,128)(2,1)S(1)}, bf16[1024,1536]{1,0:T(8,128)(2,1)}, u32[]{:S(2)}) copy-start(bf16[1024,1536]{1,0:T(8,128)(2,1)} %gate_gradient.1) | copy-start | bytes 9437188
  152.0 32.5 %collective-permute-start.12 = (bf16[512,1024]{1,0:T(8,128)(2,1)S(1)}, bf16[512,1024]{1,0:T(8,128)(2,1)S(1)}, u32[]{:S(2)}, u32[]{:S(2)}) collective-permute-start(bf16[512,1024]{1,0:T(8,128)(2,1)S(1)} %constant_dynamic-slice_fusion.10), channel_id=1, source_target_pairs={{0,2},{2,0},{4,6},{6,4},{8,10},{10,8},{12,14},{14,12},{16,18},{18,... | collective-permute-start | bytes 3145736 | tf_op jit(solution)/shard_map/ppermute | solution.py:341
  152.8 32.8 %collective-permute-start.20 = (bf16[512,1024]{1,0:T(8,128)(2,1)S(1)}, bf16[512,1024]{1,0:T(8,128)(2,1)S(1)}, u32[]{:S(2)}, u32[]{:S(2)}) collective-permute-start(bf16[512,1024]{1,0:T(8,128)(2,1)S(1)} %constant_dynamic-slice_fusion.8), channel_id=1, source_target_pairs={{0,2},{2,0},{4,6},{6,4},{8,10},{10,8},{12,14},{14,12},{16,18},{18,... | collective-permute-start | bytes 3145736 | tf_op jit(solution)/shard_map/ppermute | solution.py:341
  153.8 2.4 collective-permute-start.6
  156.2 3.7 collective-permute-start.7
  159.9 4.7 collective-permute-start.8
  164.7 81.1 %collective-permute-start.53 = (bf16[384,1024]{1,0:T(8,128)(2,1)S(1)}, bf16[384,1024]{1,0:T(8,128)(2,1)S(1)}, u32[]{:S(2)}, u32[]{:S(2)}) collective-permute-start(bf16[384,1024]{1,0:T(8,128)(2,1)S(1)} %constant_dynamic-slice_fusion.11), channel_id=1, source_target_pairs={{0,4},{2,6},{4,0},{6,2},{8,12},{10,14},{12,8},{14,10},{16,20},{18,... | collective-permute-start | bytes 2359304 | tf_op jit(solution)/shard_map/ppermute | solution.py:341
  166.2 1.2 collective-permute-start.9
  167.5 9.7 %collective-permute-start.10 = (f32[1,2304]{1,0:T(1,128)S(1)}, f32[1,2304]{1,0:T(1,128)S(1)}, u32[]{:S(2)}, u32[]{:S(2)}) collective-permute-start(f32[1,2304]{1,0:T(1,128)S(1)} %add.203), channel_id=1, source_target_pairs={{8,0},{10,2},{12,4},{14,6},{16,24},{18,26},{20,28},{22,30},{9,1},{... | collective-permute-start | bytes 27656 | tf_op jit(solution)/shard_map/ppermute | solution.py:397
  177.1 3.7 collective-permute-start.11
  180.9 66.6 %collective-permute-start.37 = (bf16[256,1536]{1,0:T(8,128)(2,1)S(1)}, bf16[256,1536]{1,0:T(8,128)(2,1)S(1)}, u32[]{:S(2)}, u32[]{:S(2)}) collective-permute-start(bf16[256,1536]{1,0:T(8,128)(2,1)S(1)} %constant_dynamic-slice_fusion.3), channel_id=1, source_target_pairs={{0,4},{2,6},{4,0},{6,2},{8,12},{10,14},{12,8},{14,10},{16,20},{18,... | collective-permute-start | bytes 2359304 | tf_op jit(solution)/shard_map/ppermute | solution.py:341
  182.5 66.5 %collective-permute-start.45 = (bf16[256,1536]{1,0:T(8,128)(2,1)S(1)}, bf16[256,1536]{1,0:T(8,128)(2,1)S(1)}, u32[]{:S(2)}, u32[]{:S(2)}) collective-permute-start(bf16[256,1536]{1,0:T(8,128)(2,1)S(1)} %constant_dynamic-slice_fusion.1), channel_id=1, source_target_pairs={{0,4},{2,6},{4,0},{6,2},{8,12},{10,14},{12,8},{14,10},{16,20},{18,... | collective-permute-start | bytes 2359304 | tf_op jit(solution)/shard_map/ppermute | solution.py:341
  184.5 45.6 %collective-permute-start.29 = (bf16[256,1024]{1,0:T(8,128)(2,1)S(1)}, bf16[256,1024]{1,0:T(8,128)(2,1)S(1)}, u32[]{:S(2)}, u32[]{:S(2)}) collective-permute-start(bf16[256,1024]{1,0:T(8,128)(2,1)S(1)} %constant_dynamic-slice_fusion.5), channel_id=1, source_target_pairs={{0,4},{2,6},{4,0},{6,2},{8,12},{10,14},{12,8},{14,10},{16,20},{18,... | collective-permute-start | bytes 1572872 | tf_op jit(solution)/shard_map/ppermute | solution.py:341
  185.6 55.8 %collective-permute-start.13 = (bf16[256,1024]{1,0:T(8,128)(2,1)S(1)}, bf16[256,1024]{1,0:T(8,128)(2,1)S(1)}, u32[]{:S(2)}, u32[]{:S(2)}) collective-permute-start(bf16[256,1024]{1,0:T(8,128)(2,1)S(1)} %constant_dynamic-slice_fusion.9), channel_id=1, source_target_pairs={{0,4},{2,6},{4,0},{6,2},{8,12},{10,14},{12,8},{14,10},{16,20},{18,... | collective-permute-start | bytes 1572872 | tf_op jit(solution)/shard_map/ppermute | solution.py:341
  230.1 20.4 %collective-permute-start.21 = (bf16[256,1024]{1,0:T(8,128)(2,1)S(1)}, bf16[256,1024]{1,0:T(8,128)(2,1)S(1)}, u32[]{:S(2)}, u32[]{:S(2)}) collective-permute-start(bf16[256,1024]{1,0:T(8,128)(2,1)S(1)} %constant_dynamic-slice_fusion.7), channel_id=1, source_target_pairs={{0,4},{2,6},{4,0},{6,2},{8,12},{10,14},{12,8},{14,10},{16,20},{18,... | collective-permute-start | bytes 1572872 | tf_op jit(solution)/shard_map/ppermute | solution.py:341
  241.4 16.5 %collective-permute-start.30 = (bf16[256,1024]{1,0:T(8,128)(2,1)S(1)}, bf16[256,1024]{1,0:T(8,128)(2,1)S(1)}, u32[]{:S(2)}, u32[]{:S(2)}) collective-permute-start(bf16[256,1024]{1,0:T(8,128)(2,1)S(1)} %add_convert_fusion.17), channel_id=1, source_target_pairs={{0,8},{2,10},{4,12},{6,14},{24,16},{26,18},{28,20},{30,22},{1,9},{... | collective-permute-start | bytes 1572872 | tf_op jit(solution)/shard_map/ppermute | solution.py:375
  245.8 23.3 %collective-permute-start.14 = (bf16[256,1024]{1,0:T(8,128)(2,1)S(1)}, bf16[256,1024]{1,0:T(8,128)(2,1)S(1)}, u32[]{:S(2)}, u32[]{:S(2)}) collective-permute-start(bf16[256,1024]{1,0:T(8,128)(2,1)S(1)} %add_convert_fusion.23), channel_id=1, source_target_pairs={{0,8},{2,10},{4,12},{6,14},{24,16},{26,18},{28,20},{30,22},{1,9},{... | collective-permute-start | bytes 1572872 | tf_op jit(solution)/shard_map/ppermute | solution.py:375
  247.4 77.1 %collective-permute-start.54 = (bf16[384,1024]{1,0:T(8,128)(2,1)S(1)}, bf16[384,1024]{1,0:T(8,128)(2,1)S(1)}, u32[]{:S(2)}, u32[]{:S(2)}) collective-permute-start(bf16[384,1024]{1,0:T(8,128)(2,1)S(1)} %add_convert_fusion.8), channel_id=1, source_target_pairs={{0,8},{2,10},{4,12},{6,14},{24,16},{26,18},{28,20},{30,22},{1,9},{... | collective-permute-start | bytes 2359304 | tf_op jit(solution)/shard_map/ppermute | solution.py:375
  249.0 76.5 %collective-permute-start.38 = (bf16[256,1536]{1,0:T(8,128)(2,1)S(1)}, bf16[256,1536]{1,0:T(8,128)(2,1)S(1)}, u32[]{:S(2)}, u32[]{:S(2)}) collective-permute-start(bf16[256,1536]{1,0:T(8,128)(2,1)S(1)} %add_convert_fusion.14), channel_id=1, source_target_pairs={{0,8},{2,10},{4,12},{6,14},{24,16},{26,18},{28,20},{30,22},{1,9},{... | collective-permute-start | bytes 2359304 | tf_op jit(solution)/shard_map/ppermute | solution.py:375
  250.6 75.9 %collective-permute-start.46 = (bf16[256,1536]{1,0:T(8,128)(2,1)S(1)}, bf16[256,1536]{1,0:T(8,128)(2,1)S(1)}, u32[]{:S(2)}, u32[]{:S(2)}) collective-permute-start(bf16[256,1536]{1,0:T(8,128)(2,1)S(1)} %add_convert_fusion.11), channel_id=1, source_target_pairs={{0,8},{2,10},{4,12},{6,14},{24,16},{26,18},{28,20},{30,22},{1,9},{... | collective-permute-start | bytes 2359304 | tf_op jit(solution)/shard_map/ppermute | solution.py:375
  257.9 65.7 %collective-permute-start.22 = (bf16[256,1024]{1,0:T(8,128)(2,1)S(1)}, bf16[256,1024]{1,0:T(8,128)(2,1)S(1)}, u32[]{:S(2)}, u32[]{:S(2)}) collective-permute-start(bf16[256,1024]{1,0:T(8,128)(2,1)S(1)} %add_convert_fusion.20), channel_id=1, source_target_pairs={{0,8},{2,10},{4,12},{6,14},{24,16},{26,18},{28,20},{30,22},{1,9},{... | collective-permute-start | bytes 1572872 | tf_op jit(solution)/shard_map/ppermute | solution.py:375
  269.1 58.2 %collective-permute-start.31 = (bf16[256,1024]{1,0:T(8,128)(2,1)S(1)}, bf16[256,1024]{1,0:T(8,128)(2,1)S(1)}, u32[]{:S(2)}, u32[]{:S(2)}) collective-permute-start(bf16[256,1024]{1,0:T(8,128)(2,1)S(1)} %add_convert_fusion.16), channel_id=1, source_target_pairs={{8,16},{10,18},{12,20},{14,22},{16,8},{18,10},{20,12},{22,14},{9,1... | collective-permute-start | bytes 1572872 | tf_op jit(solution)/shard_map/ppermute | solution.py:376
  323.6 4.7 collective-permute-start.15
  324.5 5.3 %collective-permute-start.23 = (bf16[256,1024]{1,0:T(8,128)(2,1)S(1)}, bf16[256,1024]{1,0:T(8,128)(2,1)S(1)}, u32[]{:S(2)}, u32[]{:S(2)}) collective-permute-start(bf16[256,1024]{1,0:T(8,128)(2,1)S(1)} %add_convert_fusion.19), channel_id=1, source_target_pairs={{8,16},{10,18},{12,20},{14,22},{16,8},{18,10},{20,12},{22,14},{9,1... | collective-permute-start | bytes 1572872 | tf_op jit(solution)/shard_map/ppermute | solution.py:376
  325.5 48.2 %collective-permute-start.55 = (bf16[384,1024]{1,0:T(8,128)(2,1)S(1)}, bf16[384,1024]{1,0:T(8,128)(2,1)S(1)}, u32[]{:S(2)}, u32[]{:S(2)}) collective-permute-start(bf16[384,1024]{1,0:T(8,128)(2,1)S(1)} %add_convert_fusion.7), channel_id=1, source_target_pairs={{8,16},{10,18},{12,20},{14,22},{16,8},{18,10},{20,12},{22,14},{9,1... | collective-permute-start | bytes 2359304 | tf_op jit(solution)/shard_map/ppermute | solution.py:376
  326.5 44.8 %collective-permute-start.39 = (bf16[256,1536]{1,0:T(8,128)(2,1)S(1)}, bf16[256,1536]{1,0:T(8,128)(2,1)S(1)}, u32[]{:S(2)}, u32[]{:S(2)}) collective-permute-start(bf16[256,1536]{1,0:T(8,128)(2,1)S(1)} %add_convert_fusion.13), channel_id=1, source_target_pairs={{8,16},{10,18},{12,20},{14,22},{16,8},{18,10},{20,12},{22,14},{9,1... | collective-permute-start | bytes 2359304 | tf_op jit(solution)/shard_map/ppermute | solution.py:376
  327.4 44.6 %collective-permute-start.47 = (bf16[256,1536]{1,0:T(8,128)(2,1)S(1)}, bf16[256,1536]{1,0:T(8,128)(2,1)S(1)}, u32[]{:S(2)}, u32[]{:S(2)}) collective-permute-start(bf16[256,1536]{1,0:T(8,128)(2,1)S(1)} %add_convert_fusion.10), channel_id=1, source_target_pairs={{8,16},{10,18},{12,20},{14,22},{16,8},{18,10},{20,12},{22,14},{9,1... | collective-permute-start | bytes 2359304 | tf_op jit(solution)/shard_map/ppermute | solution.py:376
  328.3 28.6 %collective-permute-start.32 = (bf16[256,1024]{1,0:T(8,128)(2,1)S(1)}, bf16[256,1024]{1,0:T(8,128)(2,1)S(1)}, u32[]{:S(2)}, u32[]{:S(2)}) collective-permute-start(bf16[256,1024]{1,0:T(8,128)(2,1)S(1)} %add_convert_fusion.15), channel_id=1, source_target_pairs={{8,0},{10,2},{12,4},{14,6},{16,24},{18,26},{20,28},{22,30},{9,1},{... | collective-permute-start | bytes 1572872 | tf_op jit(solution)/shard_map/ppermute | solution.py:380
  329.8 34.2 %collective-permute-start.16 = (bf16[256,1024]{1,0:T(8,128)(2,1)S(1)}, bf16[256,1024]{1,0:T(8,128)(2,1)S(1)}, u32[]{:S(2)}, u32[]{:S(2)}) collective-permute-start(bf16[256,1024]{1,0:T(8,128)(2,1)S(1)} %add_convert_fusion.21), channel_id=1, source_target_pairs={{8,0},{10,2},{12,4},{14,6},{16,24},{18,26},{20,28},{22,30},{9,1},{... | collective-permute-start | bytes 1572872 | tf_op jit(solution)/shard_map/ppermute | solution.py:380
  356.9 12.7 %collective-permute-start.24 = (bf16[256,1024]{1,0:T(8,128)(2,1)S(1)}, bf16[256,1024]{1,0:T(8,128)(2,1)S(1)}, u32[]{:S(2)}, u32[]{:S(2)}) collective-permute-start(bf16[256,1024]{1,0:T(8,128)(2,1)S(1)} %add_convert_fusion.18), channel_id=1, source_target_pairs={{8,0},{10,2},{12,4},{14,6},{16,24},{18,26},{20,28},{22,30},{9,1},{... | collective-permute-start | bytes 1572872 | tf_op jit(solution)/shard_map/ppermute | solution.py:380
  364.1 87.4 %collective-permute-start.34 = (bf16[256,1024]{1,0:T(8,128)(2,1)S(1)}, bf16[256,1024]{1,0:T(8,128)(2,1)S(1)}, u32[]{:S(2)}, u32[]{:S(2)}) collective-permute-start(bf16[256,1024]{1,0:T(8,128)(2,1)S(1)} %broadcast_select_fusion.3), channel_id=1, source_target_pairs={{0,2},{2,0},{4,6},{6,4},{8,10},{10,8},{12,14},{14,12},{16,18},{18,... | collective-permute-start | bytes 1572872 | tf_op jit(solution)/shard_map/ppermute | solution.py:341
  369.7 14.9 %collective-permute-start.33 = (bf16[256,1024]{1,0:T(8,128)(2,1)S(1)}, bf16[256,1024]{1,0:T(8,128)(2,1)S(1)}, u32[]{:S(2)}, u32[]{:S(2)}) collective-permute-start(bf16[256,1024]{1,0:T(8,128)(2,1)S(1)} %broadcast_select_fusion.3), channel_id=1, source_target_pairs={{0,4},{2,6},{4,0},{6,2},{8,12},{10,14},{12,8},{14,10},{16,20},{18,... | collective-permute-start | bytes 1572872 | tf_op jit(solution)/shard_map/ppermute | solution.py:341
  371.2 24.1 %collective-permute-start.17 = (bf16[256,1024]{1,0:T(8,128)(2,1)S(1)}, bf16[256,1024]{1,0:T(8,128)(2,1)S(1)}, u32[]{:S(2)}, u32[]{:S(2)}) collective-permute-start(bf16[256,1024]{1,0:T(8,128)(2,1)S(1)} %broadcast_select_fusion.5), channel_id=1, source_target_pairs={{0,4},{2,6},{4,0},{6,2},{8,12},{10,14},{12,8},{14,10},{16,20},{18,... | collective-permute-start | bytes 1572872 | tf_op jit(solution)/shard_map/ppermute | solution.py:341
  372.0 40.0 %collective-permute-start.40 = (bf16[256,1536]{1,0:T(8,128)(2,1)S(1)}, bf16[256,1536]{1,0:T(8,128)(2,1)S(1)}, u32[]{:S(2)}, u32[]{:S(2)}) collective-permute-start(bf16[256,1536]{1,0:T(8,128)(2,1)S(1)} %add_convert_fusion.12), channel_id=1, source_target_pairs={{8,0},{10,2},{12,4},{14,6},{16,24},{18,26},{20,28},{22,30},{9,1},{... | collective-permute-start | bytes 2359304 | tf_op jit(solution)/shard_map/ppermute | solution.py:380
  373.7 27.3 %collective-permute-start.25 = (bf16[256,1024]{1,0:T(8,128)(2,1)S(1)}, bf16[256,1024]{1,0:T(8,128)(2,1)S(1)}, u32[]{:S(2)}, u32[]{:S(2)}) collective-permute-start(bf16[256,1024]{1,0:T(8,128)(2,1)S(1)} %broadcast_select_fusion.4), channel_id=1, source_target_pairs={{0,4},{2,6},{4,0},{6,2},{8,12},{10,14},{12,8},{14,10},{16,20},{18,... | collective-permute-start | bytes 1572872 | tf_op jit(solution)/shard_map/ppermute | solution.py:341
  384.5 58.9 %collective-permute-start.18 = (bf16[256,1024]{1,0:T(8,128)(2,1)S(1)}, bf16[256,1024]{1,0:T(8,128)(2,1)S(1)}, u32[]{:S(2)}, u32[]{:S(2)}) collective-permute-start(bf16[256,1024]{1,0:T(8,128)(2,1)S(1)} %broadcast_select_fusion.5), channel_id=1, source_target_pairs={{0,2},{2,0},{4,6},{6,4},{8,10},{10,8},{12,14},{14,12},{16,18},{18,... | collective-permute-start | bytes 1572872 | tf_op jit(solution)/shard_map/ppermute | solution.py:341
  395.4 33.5 %collective-permute-start.48 = (bf16[256,1536]{1,0:T(8,128)(2,1)S(1)}, bf16[256,1536]{1,0:T(8,128)(2,1)S(1)}, u32[]{:S(2)}, u32[]{:S(2)}) collective-permute-start(bf16[256,1536]{1,0:T(8,128)(2,1)S(1)} %add_convert_fusion.9), channel_id=1, source_target_pairs={{8,0},{10,2},{12,4},{14,6},{16,24},{18,26},{20,28},{22,30},{9,1},{... | collective-permute-start | bytes 2359304 | tf_op jit(solution)/shard_map/ppermute | solution.py:380
  401.0 40.4 %collective-permute-start.26 = (bf16[256,1024]{1,0:T(8,128)(2,1)S(1)}, bf16[256,1024]{1,0:T(8,128)(2,1)S(1)}, u32[]{:S(2)}, u32[]{:S(2)}) collective-permute-start(bf16[256,1024]{1,0:T(8,128)(2,1)S(1)} %broadcast_select_fusion.4), channel_id=1, source_target_pairs={{0,2},{2,0},{4,6},{6,4},{8,10},{10,8},{12,14},{14,12},{16,18},{18,... | collective-permute-start | bytes 1572872 | tf_op jit(solution)/shard_map/ppermute | solution.py:341
  412.0 29.3 %collective-permute-start.56 = (bf16[384,1024]{1,0:T(8,128)(2,1)S(1)}, bf16[384,1024]{1,0:T(8,128)(2,1)S(1)}, u32[]{:S(2)}, u32[]{:S(2)}) collective-permute-start(bf16[384,1024]{1,0:T(8,128)(2,1)S(1)} %add_convert_fusion.6), channel_id=1, source_target_pairs={{8,0},{10,2},{12,4},{14,6},{16,24},{18,26},{20,28},{22,30},{9,1},{... | collective-permute-start | bytes 2359304 | tf_op jit(solution)/shard_map/ppermute | solution.py:380
  428.9 13.2 %collective-permute-start.27 = (bf16[256,1024]{1,0:T(8,128)(2,1)S(1)}, bf16[256,1024]{1,0:T(8,128)(2,1)S(1)}, u32[]{:S(2)}, u32[]{:S(2)}) collective-permute-start(bf16[256,1024]{1,0:T(8,128)(2,1)S(1)} %collective-permute-done.25), channel_id=1, source_target_pairs={{0,2},{2,0},{4,6},{6,4},{8,10},{10,8},{12,14},{14,12},{16,18},{18,... | collective-permute-start | bytes 1572872 | tf_op jit(solution)/shard_map/ppermute | solution.py:341
  441.3 3.7 collective-permute-start.19
  441.4 11.5 %collective-permute-start.35 = (bf16[256,1024]{1,0:T(8,128)(2,1)S(1)}, bf16[256,1024]{1,0:T(8,128)(2,1)S(1)}, u32[]{:S(2)}, u32[]{:S(2)}) collective-permute-start(bf16[256,1024]{1,0:T(8,128)(2,1)S(1)} %collective-permute-done.33), channel_id=1, source_target_pairs={{0,2},{2,0},{4,6},{6,4},{8,10},{10,8},{12,14},{14,12},{16,18},{18,... | collective-permute-start | bytes 1572872 | tf_op jit(solution)/shard_map/ppermute | solution.py:341
  442.0 63.9 %collective-permute-start.58 = (bf16[384,1024]{1,0:T(8,128)(2,1)S(1)}, bf16[384,1024]{1,0:T(8,128)(2,1)S(1)}, u32[]{:S(2)}, u32[]{:S(2)}) collective-permute-start(bf16[384,1024]{1,0:T(8,128)(2,1)S(1)} %broadcast_select_fusion), channel_id=1, source_target_pairs={{0,2},{2,0},{4,6},{6,4},{8,10},{10,8},{12,14},{14,12},{16,18},{18,... | collective-permute-start | bytes 2359304 | tf_op jit(solution)/shard_map/ppermute | solution.py:341
  443.5 40.8 %collective-permute-start.41 = (bf16[256,1536]{1,0:T(8,128)(2,1)S(1)}, bf16[256,1536]{1,0:T(8,128)(2,1)S(1)}, u32[]{:S(2)}, u32[]{:S(2)}) collective-permute-start(bf16[256,1536]{1,0:T(8,128)(2,1)S(1)} %broadcast_select_fusion.2), channel_id=1, source_target_pairs={{0,4},{2,6},{4,0},{6,2},{8,12},{10,14},{12,8},{14,10},{16,20},{18,... | collective-permute-start | bytes 2359304 | tf_op jit(solution)/shard_map/ppermute | solution.py:341
  445.0 35.7 %collective-permute-start.49 = (bf16[256,1536]{1,0:T(8,128)(2,1)S(1)}, bf16[256,1536]{1,0:T(8,128)(2,1)S(1)}, u32[]{:S(2)}, u32[]{:S(2)}) collective-permute-start(bf16[256,1536]{1,0:T(8,128)(2,1)S(1)} %broadcast_select_fusion.1), channel_id=1, source_target_pairs={{0,4},{2,6},{4,0},{6,2},{8,12},{10,14},{12,8},{14,10},{16,20},{18,... | collective-permute-start | bytes 2359304 | tf_op jit(solution)/shard_map/ppermute | solution.py:341
  451.4 45.7 %collective-permute-start.57 = (bf16[384,1024]{1,0:T(8,128)(2,1)S(1)}, bf16[384,1024]{1,0:T(8,128)(2,1)S(1)}, u32[]{:S(2)}, u32[]{:S(2)}) collective-permute-start(bf16[384,1024]{1,0:T(8,128)(2,1)S(1)} %broadcast_select_fusion), channel_id=1, source_target_pairs={{0,4},{2,6},{4,0},{6,2},{8,12},{10,14},{12,8},{14,10},{16,20},{18,... | collective-permute-start | bytes 2359304 | tf_op jit(solution)/shard_map/ppermute | solution.py:341
  452.9 44.9 %collective-permute-start.50 = (bf16[256,1536]{1,0:T(8,128)(2,1)S(1)}, bf16[256,1536]{1,0:T(8,128)(2,1)S(1)}, u32[]{:S(2)}, u32[]{:S(2)}) collective-permute-start(bf16[256,1536]{1,0:T(8,128)(2,1)S(1)} %broadcast_select_fusion.1), channel_id=1, source_target_pairs={{0,2},{2,0},{4,6},{6,4},{8,10},{10,8},{12,14},{14,12},{16,18},{18,... | collective-permute-start | bytes 2359304 | tf_op jit(solution)/shard_map/ppermute | solution.py:341
  480.8 17.7 %collective-permute-start.51 = (bf16[256,1536]{1,0:T(8,128)(2,1)S(1)}, bf16[256,1536]{1,0:T(8,128)(2,1)S(1)}, u32[]{:S(2)}, u32[]{:S(2)}) collective-permute-start(bf16[256,1536]{1,0:T(8,128)(2,1)S(1)} %collective-permute-done.49), channel_id=1, source_target_pairs={{0,2},{2,0},{4,6},{6,4},{8,10},{10,8},{12,14},{14,12},{16,18},{18,... | collective-permute-start | bytes 2359304 | tf_op jit(solution)/shard_map/ppermute | solution.py:341
  484.3 17.9 %collective-permute-start.42 = (bf16[256,1536]{1,0:T(8,128)(2,1)S(1)}, bf16[256,1536]{1,0:T(8,128)(2,1)S(1)}, u32[]{:S(2)}, u32[]{:S(2)}) collective-permute-start(bf16[256,1536]{1,0:T(8,128)(2,1)S(1)} %broadcast_select_fusion.2), channel_id=1, source_target_pairs={{0,2},{2,0},{4,6},{6,4},{8,10},{10,8},{12,14},{14,12},{16,18},{18,... | collective-permute-start | bytes 2359304 | tf_op jit(solution)/shard_map/ppermute | solution.py:341
  497.1 5.0 collective-permute-start.43
  497.8 8.0 %collective-permute-start.59 = (bf16[384,1024]{1,0:T(8,128)(2,1)S(1)}, bf16[384,1024]{1,0:T(8,128)(2,1)S(1)}, u32[]{:S(2)}, u32[]{:S(2)}) collective-permute-start(bf16[384,1024]{1,0:T(8,128)(2,1)S(1)} %collective-permute-done.57), channel_id=1, source_target_pairs={{0,2},{2,0},{4,6},{6,4},{8,10},{10,8},{12,14},{14,12},{16,18},{18,... | collective-permute-start | bytes 2359304 | tf_op jit(solution)/shard_map/ppermute | solution.py:341
  (14 other events, 89.4 us)
